TPU v7x, 128 devices: a whole 4x4x4 slice. The times are simulated.
128 devices in a mesh: tsec: 2 (over x_lo), dp: 32 (over y, z, core), rep: 2 (over x_hi).
Axes of the slice: x: 4 (x_hi: 2, x_lo: 2; x = x_hi * 2 + x_lo), y: 4, z: 4, core: 2. Of those that a mesh axis runs over, the one named last changes fastest.
Arguments:
- student: bfloat16 [131072, 1280], P(('dp', 'rep')), may hold values from -700 to 700
- dino_feat: bfloat16 [131072, 1536], P(('dp', 'rep'), 'tsec'), may hold values from -80 to 80
- siglip_feat: bfloat16 [131072, 1152], P(('dp', 'rep'), 'tsec'), may hold values from -80 to 80
- dino_weight: bfloat16 [1280, 1536], P(None, 'tsec'), may hold values from -0.15625 to 0.15625
- siglip_weight: bfloat16 [1280, 1152], P(None, 'tsec'), may hold values from -0.15625 to 0.15625
- send_index: int32 [131072], P(('dp', 'rep')), may hold values from 0 to 4095, as said below
- recv_index: int32 [131072], P(('dp', 'rep')), may hold values from 0 to 4095, as said below
Outputs:
- feature_grad: bfloat16 [131072, 1280], P(('dp', 'rep'))
- dino_wgrad: float32 [1280, 1536], P('dp', 'tsec')
- siglip_wgrad: float32 [1280, 1152], P('dp', 'tsec')
Inputs may be any that keep to these rules, and one draw needn't show every extreme that they name: `send_index`: on each teacher shard the 2048 values are distinct; towards each student shard a teacher shard uses exactly the slots 0 to c - 1 for some count c, and every teacher shard sends 64 rows to some student shard. All teacher shards send the same multiset of counts, some of them zero. `recv_index`: on each student shard the 2048 values are distinct and are exactly the (teacher shard, slot) pairs sent to that shard, so that every student row is paired with one teacher row and every teacher row with one student row.
All inputs are finite; a program needn't handle non-finite values.
Results may differ from a plain program's by a relative error of at most 0.018.
Values may be sent and summed in bfloat16 or wider, within the bound.
A program may use at most 128 MiB of HBM per device.

v0:
```python
import math

import jax
import jax.numpy as jnp
from jax import lax
from jax.sharding import PartitionSpec as P

E1 = 1536
E2 = 1152


norm_eps = 1e-05
length_eps = 1e-06


def for_sending(shard):
    return jax.tree.map(lambda a: a.astype(jnp.bfloat16) if a.dtype == jnp.float32 else a, shard)


def back_product(left_op, right_op):
    return lax.dot_general(
        left_op, right_op, (((1,), (1,)), ((), ())), preferred_element_type=jnp.float32
    )


def head_delta(output, target, stat_sums, head_width):
    out_sq, tgt_sq, cross = stat_sums
    out_len = jnp.sqrt(out_sq + length_eps)
    tgt_len = jnp.sqrt(tgt_sq + length_eps)
    cosine = cross / (out_len * tgt_len)
    cos_pull = (
        target / (out_len * tgt_len)[:, None] - (cosine / (out_len * out_len))[:, None] * output
    )
    return (jnp.clip(output - target, -1.0, 1.0) - head_width * cos_pull).astype(jnp.bfloat16)


def row_stats(output, target):
    return (jnp.sum(output * output, 1), jnp.sum(target * target, 1), jnp.sum(output * target, 1))


def per_device(student, dino_feat, siglip_feat, dino_weight, siglip_weight, send_index, recv_index):
    groups = lax.axis_size("dp") * lax.axis_size("rep")
    row_count = student.shape[0]
    capacity = 2 * row_count // groups
    dino_cols = dino_feat.shape[1]
    student_f = student.astype(jnp.float32)
    centred = student_f - jnp.mean(student_f, 1, keepdims=True)
    inv_dev = lax.rsqrt(jnp.mean(centred * centred, 1, keepdims=True) + norm_eps)
    normed = centred * inv_dev
    normed_bf = normed.astype(jnp.bfloat16)
    dino_out = jnp.dot(normed_bf, dino_weight, preferred_element_type=jnp.float32)
    siglip_out = jnp.dot(normed_bf, siglip_weight, preferred_element_type=jnp.float32)
    teacher = jnp.concatenate([dino_feat, siglip_feat], 1)
    row_width = teacher.shape[1]
    outbox = jnp.zeros((groups * capacity, row_width), jnp.bfloat16).at[send_index].set(teacher)
    received = lax.all_to_all(
        outbox.reshape(groups, capacity, row_width),
        ("dp", "rep"),
        split_axis=0,
        concat_axis=0,
        tiled=True,
    )
    aligned = received.reshape(groups * capacity, row_width)[recv_index].astype(jnp.float32)
    dino_target = aligned[:, :dino_cols]
    siglip_target = aligned[:, dino_cols:]
    local_stats = row_stats(dino_out, dino_target) + row_stats(siglip_out, siglip_target)
    totals = jax.tree.map(
        lambda part: part.astype(jnp.float32), lax.psum(for_sending(local_stats), "tsec")
    )
    dino_delta = head_delta(dino_out, dino_target, totals[0:3], float(E1))
    siglip_delta = head_delta(siglip_out, siglip_target, totals[3:6], float(E2))
    partial_value = back_product(dino_delta, dino_weight) + back_product(
        siglip_delta, siglip_weight
    )
    normed_grad = lax.psum(partial_value.astype(jnp.bfloat16), "tsec").astype(jnp.float32)
    grad_mean = jnp.mean(normed_grad, 1, keepdims=True)
    grad_proj = jnp.mean(normed_grad * normed, 1, keepdims=True)
    feature_grad = ((normed_grad - grad_mean - normed * grad_proj) * inv_dev).astype(jnp.bfloat16)
    row_delta = jnp.concatenate([dino_delta, siglip_delta], 1)
    full_term = lax.dot_general(
        normed_bf, row_delta, (((0,), (0,)), ((), ())), preferred_element_type=jnp.float32
    )
    summed = lax.psum(full_term.astype(jnp.bfloat16), "rep")
    weight_grad = lax.psum_scatter(summed, "dp", scatter_dimension=0, tiled=True).astype(
        jnp.float32
    )
    grad_scale = 1.0 / math.sqrt(row_count * groups)
    return (
        feature_grad,
        weight_grad[:, :dino_cols] * grad_scale,
        weight_grad[:, dino_cols:] * grad_scale,
    )


def solution(mesh):
    placed = (
        P(("dp", "rep"), None),
        P(("dp", "rep"), "tsec"),
        P(("dp", "rep"), "tsec"),
        P(None, "tsec"),
        P(None, "tsec"),
        P(("dp", "rep")),
        P(("dp", "rep")),
    )
    return jax.shard_map(
        per_device,
        mesh=mesh,
        in_specs=placed,
        out_specs=(P(("dp", "rep"), None), P("dp", "tsec"), P("dp", "tsec")),
        check_vma=False,
    )
```

profile of v0, /device:TPU:1, one launch (start us, length us, event | category | flops | bytes accessed | tf_op | source)
XLA Modules:
  0.0 472.9 jit_solution(15515282448234052582)
XLA Ops:
  8.0 4.5 copy.14
  12.5 0.7 compare_select_fusion.1
  13.2 17.0 %scatter_custom_fusion = bf16[4096,1344]{1,0:T(8,128)(2,1)} fusion(s32[2048]{0:T(1024)S(1)} %compare_select_fusion.1, bf16[2048,576]{1,0:T(8,128)(2,1)} %copy.14, bf16[]{:T(256)} %constant.33, bf16[2048,768]{1,0:T(8,128)(2,1)} %param.8, bf16[]{:T(256)} %constant.7.clone.1), kind=kCustom, calls=%fused_computation.22 | custom fusion | flops 11010048 | bytes 16515076 | tf_op jit(solution)/shard_map/scatter | solution.py:55
  30.2 12.6 %all-to-all-start = ((bf16[64,64,1344]{2,1,0:T(8,128)(2,1)}), bf16[64,64,1344]{2,1,0:T(8,128)(2,1)}, u32[]{:S(2)}, u32[]{:S(2)}) async-start(bf16[64,64,1344]{2,1,0:T(8,128)(2,1)} %bitcast.13), calls=%async_computation | async-start | bytes 23068672 | tf_op jit(solution)/shard_map/all_to_all | solution.py:56
  42.9 0.5 reduce-scatter.4.cloned.1.call-start
  43.4 3.2 convert_reduce_fusion.1
  46.6 4.0 fusion.7
  50.7 143.7 %all-to-all-done = bf16[64,64,1344]{2,1,0:T(8,128)(2,1)} async-done(((bf16[64,64,1344]{2,1,0:T(8,128)(2,1)}), bf16[64,64,1344]{2,1,0:T(8,128)(2,1)}, u32[]{:S(2)}, u32[]{:S(2)}) %all-to-all-start) | async-done | bytes 11010080 | tf_op jit(solution)/shard_map/all_to_all | solution.py:56
  194.4 18.2 %gather_fusion = bf16[2048,1344]{1,0:T(8,128)(2,1)} fusion(bf16[4096,1344]{1,0:T(8,128)(2,1)} %bitcast.1, s32[2048]{0:T(1024)S(1)} %fusion.17), kind=kCustom, calls=%fused_computation | custom fusion | bytes 11018240 | tf_op jit(solution)/shard_map/gather | solution.py:63
  212.7 8.2 %copy.15 = bf16[2048,1344]{0,1:T(8,128)(2,1)} copy(bf16[2048,1344]{1,0:T(8,128)(2,1)} %gather_fusion) | data formatting | bytes 11010048 | tf_op jit(solution)/shard_map/gather | solution.py:63
  220.9 4.3 convert_element_type.68
  225.2 8.0 %multiply_reduce_fusion.1 = (bf16[2048]{0:T(1024)(128)(2,1)S(1)}, bf16[2048]{0:T(1024)(128)(2,1)S(1)}, bf16[2048]{0:T(1024)(128)(2,1)S(1)}, f32[2048,768]{0,1:T(8,128)}) fusion(f32[2048,1344]{0,1:T(8,128)S(1)} %convert_element_type.68, bf16[1280,768]{1,0:T(8,128)(2,1)S(1)} %copy-done, bf16[2048,1280]{1,0:T(8,128)(2,1)S(1)} %bitcast.10, ...), kind=kOutput, calls=%fused_computation.20 | convolution fusion | flops 4046448640 | bytes 19820544 | tf_op jit(solution)/shard_map/dot_general | solution.py:51
  233.2 5.3 %multiply_reduce_fusion.4 = (bf16[2048]{0:T(1024)(128)(2,1)S(1)}, bf16[2048]{0:T(1024)(128)(2,1)S(1)}, bf16[2048]{0:T(1024)(128)(2,1)S(1)}, f32[2048,576]{0,1:T(8,128)}) fusion(f32[2048,1344]{0,1:T(8,128)S(1)} %convert_element_type.68, bf16[1280,576]{0,1:T(8,128)(2,1)S(1)} %copy-done.8, bf16[2048,1280]{1,0:T(8,128)(2,1)S(1)} %bitcast.10, ...), kind=kOutput, calls=%fused_computation.32 | convolution fusion | flops 3037456384 | bytes 16183296 | tf_op jit(solution)/shard_map/dot_general | solution.py:52
  238.6 8.0 %all-reduce.1 = (bf16[2048]{0:T(1024)(128)(2,1)S(1)}, bf16[2048]{0:T(1024)(128)(2,1)S(1)}, bf16[2048]{0:T(1024)(128)(2,1)S(1)}, bf16[2048]{0:T(1024)(128)(2,1)S(...) all-reduce(bf16[2048]{0:T(1024)(128)(2,1)S(1)} %get-tuple-element.6, ...), channel_id=1, replica_groups=mesh['tsec'=2,'dp'=32,'rep'=2] {'tsec'}, use_global_device_ids=true, to_apply=%region_8.0 | all-reduce | flops 12288 | bytes 49152 | tf_op jit(solution)/shard_map/psum | solution.py:68
  246.6 4.6 subtract_convert_fusion.1
  251.2 0.9 copy-done.3
  252.1 4.8 %subtract_convert_fusion = bf16[2048,768]{0,1:T(8,128)(2,1)S(1)} fusion(f32[2048,768]{0,1:T(8,128)S(1)} %copy-done.3, f32[2048,1344]{0,1:T(8,128)} %copy-done.1, f32[2048]{0:T(1024)S(1)} %get-tuple-element.23, f32[2048]{0:T(1024)S(1)} %get-tuple-element.24), kind=kLoop, calls=%fused_computation.18 | loop fusion | flops 12582912 | bytes 15745024 | tf_op jit(solution)/shard_map/convert_element_type | solution.py:34
  256.9 1.7 copy-done.4
  258.6 11.3 %convolution_convert_fusion = bf16[1280,1344]{1,0:T(8,128)(2,1)} fusion(bf16[2048,576]{0,1:T(8,128)(2,1)S(1)} %subtract_convert_fusion.1, bf16[2048,768]{0,1:T(8,128)(2,1)S(1)} %subtract_convert_fusion, bf16[2048,1280]{1,0:T(8,128)(2,1)S(1)} %bitcast.12, f32[2048]{0:T(1024)S(1)} %add_rsqrt_fusion, f32[2048]{0:T(1024)S(1)} %broadcast_multiply_fusion.2), kind=kOutput, calls=%fused_computation.17 | convolution fusion | flops 7069646848 | bytes 14204928 | tf_op jit(solution)/shard_map/dot_general | solution.py:80
  270.0 0.3 all-reduce.5.cloned.1.call-start
  270.3 6.4 %fusion.24 = f32[2048,1280]{1,0:T(8,128)S(1)} fusion(bf16[2048,768]{0,1:T(8,128)(2,1)} %copy-done.4, bf16[1280,768]{1,0:T(8,128)(2,1)S(1)} %copy-done), kind=kOutput, calls=%fused_computation.52 | convolution fusion | flops 4026531840 | bytes 15597568 | tf_op jit(solution)/shard_map/dot_general | solution.py:21
  276.7 6.0 %add_convert_fusion = bf16[2048,1280]{1,0:T(8,128)(2,1)} fusion(f32[2048,1280]{1,0:T(8,128)S(1)} %fusion.24, bf16[2048,576]{0,1:T(8,128)(2,1)S(1)} %copy-done.6, bf16[1280,576]{0,1:T(8,128)(2,1)S(1)} %copy-done.9), kind=kOutput, calls=%fused_computation.16 | convolution fusion | flops 3025141760 | bytes 19562496 | tf_op jit(solution)/shard_map/dot_general | solution.py:21
  282.7 0.0 all-reduce.5.cloned.1.call-update
  282.7 0.0 all-reduce.7.cloned.1.call-start
  282.8 82.8 %reduce-scatter.4.cloned.1.call-done = bf16[40,1344]{1,0:T(8,128)(2,1)} async-done(((bf16[1280,1344]{1,0:T(8,128)(2,1)}), bf16[40,1344]{1,0:T(8,128)(2,1)}) %reduce-scatter.4.cloned.1.call-update) | async-done | bytes 107536
  365.6 65.5 %all-reduce.5.cloned.1.call-done = bf16[2048,1280]{1,0:T(8,128)(2,1)} async-done(((bf16[2048,1280]{1,0:T(8,128)(2,1)}), bf16[2048,1280]{1,0:T(8,128)(2,1)}) %all-reduce.5.cloned.1.call-update) | async-done | bytes 5242896 | tf_op jit(solution)/shard_map/psum | solution.py:75
  431.1 7.8 %convert_reduce_fusion = (f32[2048]{0:T(1024)S(1)}, f32[2048]{0:T(1024)S(1)}) fusion(bf16[2048,1280]{1,0:T(8,128)(2,1)} %all-reduce.5.cloned.1.call-done, f32[2048]{0:T(1024)S(1)} %add_rsqrt_fusion, f32[2048]{0:T(1024)S(1)} %broadcast_multiply_fusion.2, bf16[2048,1280]{1,0:T(8,128)(2,1)} %param.7), kind=kLoop, calls=%fused_computation.4 | loop fusion | flops 18345984 | bytes 10518528 | tf_op jit(solution)/shard_map/reduce_sum | solution.py:76
  438.9 7.1 %fusion.6 = bf16[2048,1280]{1,0:T(8,128)(2,1)} fusion(bf16[2048,1280]{1,0:T(8,128)(2,1)} %param.7, bf16[2048,1280]{1,0:T(8,128)(2,1)S(1)} %copy-done.2, f32[2048]{0:T(1024)S(1)} %broadcast_multiply_fusion, f32[2048]{0:T(1024)S(1)} %broadcast_multiply_fusion.1, f32[2048]{0:T(1024)S(1)} %add_rsqrt_fusion, f32[2048]{0:T(1024)S(1)} %broadcast_multiply_fusion.2), kind=kLoop, calls=%fused_computation.13 | loop fusion | flops 23592960 | bytes 15761408 | tf_op jit(solution)/shard_map/convert_element_type | solution.py:78
  446.1 17.0 %all-reduce.7.cloned.1.call-done = bf16[40,1344]{1,0:T(8,128)(2,1)} async-done(((bf16[40,1344]{1,0:T(8,128)(2,1)}), bf16[40,1344]{1,0:T(8,128)(2,1)}) %all-reduce.7.cloned.1.call-update) | async-done | bytes 107536 | tf_op jit(solution)/shard_map/psum | solution.py:83
  463.0 0.9 convert_element_type.87
  463.9 0.7 slice_multiply_fusion
  464.6 0.7 slice_multiply_fusion.1
  (36 shorter events, 0.2 us)
Async XLA Ops:
  8.0 217.1 %copy-start = (bf16[1280,768]{1,0:T(8,128)(2,1)S(1)}, bf16[1280,768]{1,0:T(8,128)(2,1)}, u32[]{:S(2)}) copy-start(bf16[1280,768]{1,0:T(8,128)(2,1)} %param.10) | copy-start | bytes 5898244
  30.2 164.2 %all-to-all-start = ((bf16[64,64,1344]{2,1,0:T(8,128)(2,1)}), bf16[64,64,1344]{2,1,0:T(8,128)(2,1)}, u32[]{:S(2)}, u32[]{:S(2)}) async-start(bf16[64,64,1344]{2,1,0:T(8,128)(2,1)} %bitcast.13), calls=%async_computation | async-start | bytes 23068672 | tf_op jit(solution)/shard_map/all_to_all | solution.py:56
  42.9 7.8 %copy-start.7 = (s32[2048]{0:T(1024)S(1)}, s32[2048]{0:T(1024)}, u32[]{:S(2)}) copy-start(s32[2048]{0:T(1024)} %param.13) | copy-start | bytes 24580
  42.9 322.7 %reduce-scatter.4.cloned.1.call-start = ((), (), s32[]{:S(2)}) async-start(), calls=%async_computation.4 | async-start | bytes 3717120
  212.6 12.5 %slice-start = ((s8[5242880]{0:T(1024)(128)(4,1)}), s8[1048576]{0:T(1024)(128)(4,1)S(1)}, s32[]{:S(2)}) async-start(s8[5242880]{0:T(1024)(128)(4,1)} %bitcast.9), calls=%async_computation.5 | async-start | bytes 2097152
  220.9 4.3 slice-start.1
  225.2 8.1 %copy-start.1 = (f32[2048,1344]{0,1:T(8,128)}, f32[2048,1344]{0,1:T(8,128)S(1)}, u32[]{:S(2)}) copy-start(f32[2048,1344]{0,1:T(8,128)S(1)} %convert_element_type.68) | copy-start | bytes 33030148
  225.2 8.1 %copy-start.8 = (bf16[1280,576]{0,1:T(8,128)(2,1)S(1)}, bf16[1280,576]{0,1:T(8,128)(2,1)}, u32[]{:S(2)}) copy-start(bf16[1280,576]{0,1:T(8,128)(2,1)} %param.11) | copy-start | bytes 4423684
  246.6 5.5 %copy-start.3 = (f32[2048,768]{0,1:T(8,128)S(1)}, f32[2048,768]{0,1:T(8,128)}, u32[]{:S(2)}) copy-start(f32[2048,768]{0,1:T(8,128)} %get-tuple-element.21) | copy-start | bytes 18874372
  246.6 12.0 %slice-start.2 = ((s8[5242880]{0:T(1024)(128)(4,1)}), s8[4194304]{0:T(1024)(128)(4,1)S(1)}, s32[]{:S(2)}) async-start(s8[5242880]{0:T(1024)(128)(4,1)} %bitcast.11), calls=%async_computation.7 | async-start | bytes 8388608
  251.2 5.7 %copy-start.5 = (bf16[2048,576]{0,1:T(8,128)(2,1)}, bf16[2048,576]{0,1:T(8,128)(2,1)S(1)}, u32[]{:S(2)}) copy-start(bf16[2048,576]{0,1:T(8,128)(2,1)S(1)} %subtract_convert_fusion.1) | copy-start | bytes 7077892
  252.1 6.5 %slice-start.3 = ((s8[5242880]{0:T(1024)(128)(4,1)}), s8[1048576]{0:T(1024)(128)(4,1)S(1)}, s32[]{:S(2)}) async-start(s8[5242880]{0:T(1024)(128)(4,1)} %bitcast.11), calls=%async_computation.8 | async-start | bytes 2097152
  256.9 1.7 copy-start.4
  270.0 161.1 %all-reduce.5.cloned.1.call-start = ((), (), s32[]{:S(2)}) async-start(), calls=%async_computation.2 | async-start | bytes 10485760 | tf_op jit(solution)/shard_map/psum | solution.py:75
  270.2 6.4 %copy-start.6 = (bf16[2048,576]{0,1:T(8,128)(2,1)S(1)}, bf16[2048,576]{0,1:T(8,128)(2,1)}, u32[]{:S(2)}) copy-start(bf16[2048,576]{0,1:T(8,128)(2,1)} %copy-done.5) | copy-start | bytes 7077892
  270.2 6.4 %copy-start.9 = (bf16[1280,576]{0,1:T(8,128)(2,1)S(1)}, bf16[1280,576]{0,1:T(8,128)(2,1)}, u32[]{:S(2)}) copy-start(bf16[1280,576]{0,1:T(8,128)(2,1)} %param.11) | copy-start | bytes 4423684
  282.7 180.3 %all-reduce.7.cloned.1.call-start = ((), (), s32[]{:S(2)}) async-start(), calls=%async_computation.3 | async-start | bytes 225280 | tf_op jit(solution)/shard_map/psum | solution.py:83
  431.1 7.9 %copy-start.2 = (bf16[2048,1280]{1,0:T(8,128)(2,1)S(1)}, bf16[2048,1280]{1,0:T(8,128)(2,1)}, u32[]{:S(2)}) copy-start(bf16[2048,1280]{1,0:T(8,128)(2,1)} %all-reduce.5.cloned.1.call-done) | copy-start | bytes 15728644
Sparse Core Ops, SparseCore 0:
  270.1 95.3 reduce-scatter.3
Sparse Core Ops, SparseCore 1:
  282.8 148.2 all-reduce.4
  433.3 29.6 all-reduce.6
where the time goes:
time: 481 us; the launch traced here: 473 us
  waiting for transfers between devices  309 us (64%)
  other arithmetic  55.9 us (12%)
  matrix products  37.1 us (8%)
  local copies, waits for them, and re-layouts  33.5 us (7%)
  between operations  16 us (3%)
  starting transfers between devices  13.4 us (3%)
  blocking collectives  7.95 us (2%)
    all_to_all x1, waiting for transfers between devices, per_device(): lax.all_to_all(outbox.reshape(groups, capacity, row_width), ('dp', 'rep')...  144 us
    unnamed x4, waiting for transfers between devices  82.8 us
    psum x1, waiting for transfers between devices, per_device(): lax.psum(partial_value.astype(jnp.bfloat16), 'tsec').astype(jnp.float32)  65.5 us
    gather x2, local copies, waits for them, and re-layouts, per_device(): received.reshape(groups * capacity, row_width)[recv_index]  26.5 us
    scatter x1, other arithmetic, per_device(): jnp.zeros((groups * capacity, row_width), jnp.bfloat16).at[send_index]  17 us
    psum x1, waiting for transfers between devices, per_device(): summed = lax.psum(full_term.astype(jnp.bfloat16), 'rep')  17 us
    all_to_all x1, starting transfers between devices, per_device(): lax.all_to_all(outbox.reshape(groups, capacity, row_width), ('dp', 'rep')...  12.6 us
    dot_general x2, matrix products, back_product(): lax.dot_general(left_op, right_op, (((1,), (1,)), ((), ())), preferred_el...  12.4 us
  transfers between devices with their start and end apart: 4, of which 4 were waited for; matrix products, arithmetic and copies ran while one was open for 7% of the time, Pallas kernels for 0%

commit v1 on v0

v1 whole, which is shorter than its diff:
```python
import math

import jax
import jax.numpy as jnp
from jax import lax
from jax.experimental import pallas as pl
from jax.experimental.pallas import tpu as pltpu
from jax.sharding import PartitionSpec as P

E1 = 1536
E2 = 1152
CHUNKS = ((0, 32), (32, 32))

norm_eps = 1e-05
length_eps = 1e-06
MESH = pl.DeviceIdType.MESH
BF = jnp.bfloat16
F32 = jnp.float32


def exact_pick(hit, table):
    return jnp.dot(hit.astype(BF), table, preferred_element_type=F32).astype(BF)


def back_product(left_op, right_op):
    return lax.dot_general(
        left_op, right_op, (((1,), (1,)), ((), ())), preferred_element_type=F32
    )


def outer_product(left_op, right_op):
    return lax.dot_general(
        left_op, right_op, (((0,), (0,)), ((), ())), preferred_element_type=F32
    )


def head_delta(outputs, targets, head_width):
    out_sq = sum(jnp.sum(y * y, 1, keepdims=True) for y in outputs)
    tgt_sq = sum(jnp.sum(f * f, 1, keepdims=True) for f in targets)
    cross = sum(jnp.sum(y * f, 1, keepdims=True) for y, f in zip(outputs, targets))
    out_len = jnp.sqrt(out_sq + length_eps)
    tgt_len = jnp.sqrt(tgt_sq + length_eps)
    cosine = cross / (out_len * tgt_len)
    pull_f = head_width / (out_len * tgt_len)
    pull_y = head_width * cosine / (out_len * out_len)
    return [
        (jnp.clip(y - f, -1.0, 1.0) - (pull_f * f - pull_y * y)).astype(BF)
        for y, f in zip(outputs, targets)
    ]


def place():
    dp = lax.axis_index("dp")
    x = lax.axis_index("rep") * 2 + lax.axis_index("tsec")
    return x, dp // 8, (dp // 2) % 4, dp % 2


def at_place(x, y, z, c):
    return {"tsec": x % 2, "dp": (y * 4 + z) * 2 + c, "rep": x // 2}


def sum_kernel(part_ref, out_ref, held, pair, far_y, far_z, far_y2, far_z2, far_x, stage,
               own_sem, pair_send, pair_recv, send_sem, recv_sem):
    x, y, z, c = place()
    t = x % 2
    barrier = pltpu.get_barrier_semaphore()

    def greet(device):
        pl.semaphore_signal(barrier, inc=1, device_id=device, device_id_type=MESH)

    greet(at_place(x, y, z, 1 - c))
    for j in (1, 2, 3):
        greet(at_place(x, (y + j) % 4, z, c))
        greet(at_place(x, y, (z + j) % 4, c))
        greet(at_place((x + j) % 4, y, z, c))
    pl.semaphore_wait(barrier, 10)

    order = (2, 1, 3, 0)

    def pair_copy(k, j, i):
        line = (y + j) % 4 if k == 0 else (z + j) % 4
        src = part_ref.at[0, line, :, 1 - c] if k == 0 else part_ref.at[1, :, line, 1 - c]
        return pltpu.make_async_remote_copy(
            src_ref=src, dst_ref=pair.at[k, j], send_sem=pair_send.at[i], recv_sem=pair_recv.at[i],
            device_id=at_place(x, y, z, 1 - c), device_id_type=MESH)

    def own_copy(k, j, i):
        line = (y + j) % 4 if k == 0 else (z + j) % 4
        src = part_ref.at[0, line, :, c] if k == 0 else part_ref.at[1, :, line, c]
        return pltpu.make_async_copy(src, held.at[k, j], own_sem.at[i])

    def line_copy(k, j, i):
        far = far_y if k == 0 else far_z
        device = at_place(x, (y + j) % 4, z, c) if k == 0 else at_place(x, y, (z + j) % 4, c)
        return pltpu.make_async_remote_copy(
            src_ref=held.at[k, j], dst_ref=far.at[j - 1], send_sem=send_sem.at[i], recv_sem=recv_sem.at[i],
            device_id=device, device_id_type=MESH)

    steps = [(k, j) for j in order for k in (0, 1)]
    for i, (k, j) in enumerate(steps):
        pair_copy(k, j, i).start()
        own_copy(k, j, i).start()
    for i, (k, j) in enumerate(steps):
        own_copy(k, j, i).wait()
        pair_copy(k, j, i).wait_recv()

        @pl.loop(0, 4)
        def _(b, k=k, j=j):
            held[k, j, b] = (held[k, j, b].astype(F32) + pair[k, j, b].astype(F32)).astype(BF)

        if j:
            line_copy(k, j, k * 3 + j - 1).start()
    for i, (k, j) in enumerate(steps):
        pair_copy(k, j, i).wait_send()
    for k in (0, 1):
        for j in (2, 1, 3):
            line_copy(k, j, k * 3 + j - 1).wait()
        far = far_y if k == 0 else far_z

        @pl.loop(0, 4)
        def _(b, k=k, far=far):
            held[k, 0, b] = (held[k, 0, b].astype(F32) + far[0, b].astype(F32)
                             + far[1, b].astype(F32) + far[2, b].astype(F32)).astype(BF)

    def cross_copy(k, j):
        far = far_z2 if k == 0 else far_y2
        b = (z + j) % 4 if k == 0 else (y + j) % 4
        device = at_place(x, y, b, c) if k == 0 else at_place(x, b, z, c)
        i = 6 + k * 3 + j - 1
        return pltpu.make_async_remote_copy(
            src_ref=held.at[k, 0, b], dst_ref=far.at[j - 1], send_sem=send_sem.at[i], recv_sem=recv_sem.at[i],
            device_id=device, device_id_type=MESH)

    for k in (0, 1):
        for j in (2, 1, 3):
            cross_copy(k, j).start()
    for k in (0, 1):
        for j in (2, 1, 3):
            cross_copy(k, j).wait()
        far = far_z2 if k == 0 else far_y2
        mine = held[k, 0, z] if k == 0 else held[k, 0, y]
        stage[k] = (mine.astype(F32) + far[0].astype(F32) + far[1].astype(F32) + far[2].astype(F32)).astype(BF)

    def x_copy(j):
        device = (x + j) % 4
        i = 12 + j - 1
        return pltpu.make_async_remote_copy(
            src_ref=stage.at[device % 2], dst_ref=far_x.at[j - 1], send_sem=send_sem.at[i], recv_sem=recv_sem.at[i],
            device_id=at_place(device, y, z, c), device_id_type=MESH)

    for j in (2, 1, 3):
        x_copy(j).start()
    for j in (2, 1, 3):
        x_copy(j).wait()
    out_ref[...] = (stage[t].astype(F32) + far_x[0].astype(F32) + far_x[1].astype(F32) + far_x[2].astype(F32))


def sum_parts(part):
    rows, width = part.shape[-2:]
    block = (rows, width)
    return pl.pallas_call(
        sum_kernel,
        out_shape=jax.ShapeDtypeStruct(block, F32),
        in_specs=[pl.BlockSpec(memory_space=pl.ANY)],
        out_specs=pl.BlockSpec(memory_space=pltpu.VMEM),
        scratch_shapes=[
            pltpu.VMEM((2, 4, 4) + block, BF),
            pltpu.VMEM((2, 4, 4) + block, BF),
            pltpu.VMEM((3, 4) + block, BF),
            pltpu.VMEM((3, 4) + block, BF),
            pltpu.VMEM((3,) + block, BF),
            pltpu.VMEM((3,) + block, BF),
            pltpu.VMEM((3,) + block, BF),
            pltpu.VMEM((2,) + block, BF),
            pltpu.SemaphoreType.DMA((8,)),
            pltpu.SemaphoreType.DMA((8,)),
            pltpu.SemaphoreType.DMA((8,)),
            pltpu.SemaphoreType.DMA((15,)),
            pltpu.SemaphoreType.DMA((15,)),
        ],
        compiler_params=pltpu.CompilerParams(
            collective_id=0, has_side_effects=True, vmem_limit_bytes=40 * 2**20
        ),
    )(part)


def per_device(student, dino_feat, siglip_feat, dino_weight, siglip_weight, send_index, recv_index):
    groups = lax.axis_size("dp") * lax.axis_size("rep")
    row_count = student.shape[0]
    capacity = 2 * row_count // groups
    dino_cols = dino_feat.shape[1]
    t = lax.axis_index("tsec")
    rep = lax.axis_index("rep")
    first = t == 0
    swap = [(0, 1), (1, 0)]
    n_dp = lax.axis_size("dp")
    mirrored = [
        [((tt ^ r) * n_dp + d) * 2 + r for d in range(n_dp) for r in range(2)] for tt in range(2)
    ]

    teacher = jnp.concatenate([dino_feat, siglip_feat], 1)
    weight_own = jnp.concatenate([dino_weight, siglip_weight], 1)
    weight_far = lax.ppermute(weight_own, "tsec", swap)
    weights = (jnp.where(first, weight_own, weight_far), jnp.where(first, weight_far, weight_own))

    def slot_codes(start, size):
        group = lax.broadcasted_iota(jnp.int32, (groups, size), 0)
        slot = lax.broadcasted_iota(jnp.int32, (groups, size), 1)
        return (group * capacity + slot + start).reshape(-1)

    inboxes = []
    for start, size in CHUNKS:
        codes = slot_codes(start, size)
        outbox = exact_pick(codes[:, None] == send_index[None, :], teacher)
        arrived = lax.all_to_all(
            outbox.reshape(groups, size, -1),
            ("tsec", "dp", "rep"),
            split_axis=0,
            concat_axis=0,
            axis_index_groups=mirrored,
            tiled=True,
        )
        inboxes.append((codes, arrived.reshape(groups * size, -1)))

    key = (recv_index % capacity) * groups + recv_index // capacity
    rank = jnp.sum((key[:, None] > key[None, :]).astype(jnp.int32), 1)
    ranks = jnp.arange(row_count, dtype=jnp.int32)
    code_at = jnp.sum(jnp.where(rank[None, :] == ranks[:, None], recv_index[None, :], 0), 1)

    wgrads = [0.0, 0.0]
    feature_grad = 0.0
    for index, (start, size) in enumerate(CHUNKS):
        begin = row_count * start // capacity
        half = row_count * size // capacity // 2
        mine = begin + t * half
        other = begin + (1 - t) * half
        code_mine = lax.dynamic_slice(code_at, (mine,), (half,))
        code_other = lax.dynamic_slice(code_at, (other,), (half,))

        def aligned(code):
            total = 0
            for codes, rows in inboxes[: index + 1]:
                total = total + exact_pick(code[:, None] == codes[None, :], rows)
            return total

        near = aligned(code_mine)
        far = lax.ppermute(aligned(code_other), "tsec", swap)
        direct = (((code_mine // capacity) % 2 == rep) == first)[:, None]
        halves = [jnp.where(direct, near, far).astype(F32), jnp.where(direct, far, near).astype(F32)]

        pos_mine = mine + jnp.arange(half, dtype=jnp.int32)
        pos_other = other + jnp.arange(half, dtype=jnp.int32)
        student_f = exact_pick(pos_mine[:, None] == rank[None, :], student).astype(F32)
        centred = student_f - jnp.mean(student_f, 1, keepdims=True)
        inv_dev = lax.rsqrt(jnp.mean(centred * centred, 1, keepdims=True) + norm_eps)
        normed = centred * inv_dev
        normed_bf = normed.astype(BF)
        outs = [jnp.dot(normed_bf, w, preferred_element_type=F32) for w in weights]
        dino = head_delta([y[:, :dino_cols] for y in outs], [f[:, :dino_cols] for f in halves], float(E1))
        siglip = head_delta([y[:, dino_cols:] for y in outs], [f[:, dino_cols:] for f in halves], float(E2))
        deltas = [jnp.concatenate([d, s], 1) for d, s in zip(dino, siglip)]
        wgrads = [g + outer_product(normed_bf, d) for g, d in zip(wgrads, deltas)]
        normed_grad = sum(back_product(d, w).astype(BF).astype(F32) for d, w in zip(deltas, weights))
        grad_mean = jnp.mean(normed_grad, 1, keepdims=True)
        grad_proj = jnp.mean(normed_grad * normed, 1, keepdims=True)
        grad = ((normed_grad - grad_mean - normed * grad_proj) * inv_dev).astype(BF)
        grad_far = lax.ppermute(grad, "tsec", swap)
        feature_grad = feature_grad + exact_pick(rank[:, None] == pos_mine[None, :], grad)
        feature_grad = feature_grad + exact_pick(rank[:, None] == pos_other[None, :], grad_far)

    owners = lax.axis_size("dp")
    part = jnp.stack([
        jnp.pad(g.reshape(owners, -1, g.shape[1]), ((0, 0), (0, 8), (0, 0))).astype(BF) for g in wgrads
    ])
    own_rows = student.shape[1] // owners
    part = part.reshape((2, 4, 4, 2) + part.shape[2:])
    grad_scale = 1.0 / math.sqrt(row_count * groups)
    weight_grad = sum_parts(part)[:own_rows] * grad_scale
    return feature_grad, weight_grad[:, :dino_cols], weight_grad[:, dino_cols:]


def solution(mesh):
    placed = (
        P(("dp", "rep"), None),
        P(("dp", "rep"), "tsec"),
        P(("dp", "rep"), "tsec"),
        P(None, "tsec"),
        P(None, "tsec"),
        P(("dp", "rep")),
        P(("dp", "rep")),
    )
    return jax.shard_map(
        per_device,
        mesh=mesh,
        in_specs=placed,
        out_specs=(P(("dp", "rep"), None), P("dp", "tsec"), P("dp", "tsec")),
        check_vma=False,
    )
```

time: 481 us -> 453 us (0.942)
  waiting for transfers between devices: 309 us -> 125 us
  matrix products: 37.1 us -> 146 us
  Pallas kernels: 0 us -> 52.5 us
  starting transfers between devices: 13.4 us -> 44.2 us
  other arithmetic: 55.9 us -> 27.4 us
  local copies, waits for them, and re-layouts: 33.5 us -> 48.9 us
  between operations: 16 us -> 1.67 us
  blocking collectives: 7.95 us -> 0 us
    dot_general x3 -> x22, matrix products: 24.7 us -> 134 us  [the longest x14 101 us: exact_pick(): return jnp.dot(hit.astype(BF), table, preferred_element_type=F32).astype(BF)]
    unnamed x4 -> x0, waiting for transfers between devices: 82.8 us -> none
    psum x2 -> x0, waiting for transfers between devices: 82.5 us -> none  [the longest x1 65.5 us: per_device(): lax.psum(partial_value.astype(jnp.bfloat16), 'tsec').astype(jnp.float32)]
    all_to_all x1 -> x2, waiting for transfers between devices: 144 us -> 69.1 us  [per_device(): lax.all_to_all(outbox.reshape(groups, size, -1), ('tsec', 'dp', 'rep'), s...]
    ppermute x0 -> x5, waiting for transfers between devices: none -> 55.5 us  [the longest x2 38.3 us: per_device(): far = lax.ppermute(aligned(code_other), 'tsec', swap)]
    pallas_call x0 -> x1, Pallas kernels: none -> 52.5 us  [sum_parts(): pl.pallas_call(sum_kernel, out_shape=jax.ShapeDtypeStruct(block, F32), in...]
    gather x2 -> x0, local copies, waits for them, and re-layouts: 26.5 us -> none  [per_device(): received.reshape(groups * capacity, row_width)[recv_index]]
    all_to_all x1 -> x2, starting transfers between devices: 12.6 us -> 36.7 us  [per_device(): lax.all_to_all(outbox.reshape(groups, size, -1), ('tsec', 'dp', 'rep'), s...]
  transfers between devices with their start and end apart: 4 -> 7, of which waited for: 4 -> 5; matrix products, arithmetic and copies ran while one was open for 7% -> 39% of each run, Pallas kernels for 0% -> 12%
where the time goes in v1:
time: 453 us; the launch traced here: 445 us
  matrix products  146 us (32%)
  waiting for transfers between devices  125 us (28%)
  Pallas kernels  52.5 us (12%)
  local copies, waits for them, and re-layouts  48.9 us (11%)
  starting transfers between devices  44.2 us (10%)
  other arithmetic  27.4 us (6%)
    dot_general x14, matrix products, exact_pick(): return jnp.dot(hit.astype(BF), table, preferred_element_type=F32).astype(BF)  101 us
    all_to_all x2, waiting for transfers between devices, per_device(): lax.all_to_all(outbox.reshape(groups, size, -1), ('tsec', 'dp', 'rep'), s...  69.1 us
    pallas_call x1, Pallas kernels, sum_parts(): pl.pallas_call(sum_kernel, out_shape=jax.ShapeDtypeStruct(block, F32), in...  52.5 us
    ppermute x2, waiting for transfers between devices, per_device(): far = lax.ppermute(aligned(code_other), 'tsec', swap)  38.3 us
    all_to_all x2, starting transfers between devices, per_device(): lax.all_to_all(outbox.reshape(groups, size, -1), ('tsec', 'dp', 'rep'), s...  36.7 us
    dot_general x4, matrix products, outer_product(): lax.dot_general(left_op, right_op, (((0,), (0,)), ((), ())), preferred_el...  18.1 us
    ppermute x2, waiting for transfers between devices, per_device(): grad_far = lax.ppermute(grad, 'tsec', swap)  17.2 us
    convert_element_type x2, local copies, waits for them, and re-layouts, exact_pick(): return jnp.dot(hit.astype(BF), table, preferred_element_type=F32).astype(BF)  16.9 us
  transfers between devices with their start and end apart: 7, of which 5 were waited for; matrix products, arithmetic and copies ran while one was open for 39% of the time, Pallas kernels for 12%

profile of v1, /device:TPU:1, one launch (start us, length us, event | category | flops | bytes accessed | tf_op | source)
XLA Modules:
  0.0 445.2 jit_solution(10744022395734505136)
XLA Ops:
  11.2 16.0 %fusion.8 = bf16[2048,1344]{0,1:T(8,128)(2,1)} fusion(s32[2048]{0:T(1024)S(1)} %copy-done.26, s32[2048]{0:T(1024)S(1)} %add.422, bf16[2048,576]{1,0:T(8,128)(2,1)S(1)} %copy.27, bf16[2048,768]{1,0:T(8,128)(2,1)} %param.8), kind=kOutput, calls=%fused_computation.14 | convolution fusion | flops 11292246016 | bytes 11026432 | tf_op jit(solution)/shard_map/dot_general | solution.py:22
  27.1 8.3 %copy.28 = bf16[2048,1344]{1,0:T(8,128)(2,1)} copy(bf16[2048,1344]{0,1:T(8,128)(2,1)} %fusion.8) | data formatting | bytes 11010048 | tf_op jit(solution)/shard_map/convert_element_type | solution.py:22
  35.4 11.5 %all-to-all-start = ((bf16[64,32,1344]{2,1,0:T(8,128)(2,1)}), bf16[64,32,1344]{2,1,0:T(8,128)(2,1)}, u32[]{:S(2)}, u32[]{:S(2)}) async-start(bf16[64,32,1344]{2,1,0:T(8,128)(2,1)} %bitcast.28), calls=%async_computation | async-start | bytes 11534336 | tf_op jit(solution)/shard_map/all_to_all | solution.py:215
  47.0 16.0 %fusion.11 = bf16[2048,1344]{0,1:T(8,128)(2,1)} fusion(s32[2048]{0:T(1024)S(1)} %copy-done.26, s32[2048]{0:T(1024)S(1)} %broadcast_add_fusion, bf16[2048,576]{1,0:T(8,128)(2,1)S(1)} %copy.27, bf16[2048,768]{1,0:T(8,128)(2,1)} %param.8), kind=kOutput, calls=%fused_computation.15 | convolution fusion | flops 11292246016 | bytes 11026432 | tf_op jit(solution)/shard_map/dot_general | solution.py:22
  63.0 8.7 %copy.29 = bf16[2048,1344]{1,0:T(8,128)(2,1)} copy(bf16[2048,1344]{0,1:T(8,128)(2,1)} %fusion.11) | data formatting | bytes 11010048 | tf_op jit(solution)/shard_map/convert_element_type | solution.py:22
  76.5 5.5 %convert_reduce_fusion.1 = (f32[512]{0:T(512)S(1)}, bf16[512,1280]{1,0:T(8,128)(2,1)S(1)}) fusion(bf16[2048,1280]{1,0:T(8,128)(2,1)} %param.7, s32[2048]{0:T(1024)S(1)} %convert_reduce_fusion, s32[512]{0:T(512)S(1)} %iota_add_fusion.2), kind=kOutput, calls=%fused_computation.50 | convolution fusion | flops 2687368704 | bytes 6565888 | tf_op jit(solution)/shard_map/dot_general | solution.py:22
  83.5 5.5 %convert_reduce_fusion.2 = (f32[512]{0:T(512)S(1)}, bf16[512,1280]{1,0:T(8,128)(2,1)S(1)}) fusion(bf16[2048,1280]{1,0:T(8,128)(2,1)} %param.7, s32[2048]{0:T(1024)S(1)} %convert_reduce_fusion, s32[512]{0:T(512)S(1)} %iota_add_fusion.4), kind=kOutput, calls=%fused_computation.52 | convolution fusion | flops 2687368704 | bytes 6565888 | tf_op jit(solution)/shard_map/dot_general | solution.py:22
  89.0 27.3 %all-to-all-done = bf16[64,32,1344]{2,1,0:T(8,128)(2,1)} async-done(((bf16[64,32,1344]{2,1,0:T(8,128)(2,1)}), bf16[64,32,1344]{2,1,0:T(8,128)(2,1)}, u32[]{:S(2)}, u32[]{:S(2)}) %all-to-all-start) | async-done | bytes 5505056 | tf_op jit(solution)/shard_map/all_to_all | solution.py:215
  116.3 25.2 %all-to-all-start.1 = ((bf16[64,32,1344]{2,1,0:T(8,128)(2,1)}), bf16[64,32,1344]{2,1,0:T(8,128)(2,1)}, u32[]{:S(2)}, u32[]{:S(2)}) async-start(bf16[64,32,1344]{2,1,0:T(8,128)(2,1)} %bitcast.29), calls=%async_computation.1 | async-start | bytes 11534336 | tf_op jit(solution)/shard_map/all_to_all | solution.py:215
  149.6 3.8 fusion.149
  160.8 8.4 %fusion.73 = bf16[512,1344]{0,1:T(8,128)(2,1)} fusion(bf16[2048,1344]{1,0:T(8,128)(2,1)} %bitcast.1, s32[2048]{0:T(1024)S(1)} %add.422, s32[512]{0:T(512)S(1)} %get-tuple-element.48), kind=kOutput, calls=%fused_computation.79 | convolution fusion | flops 2820308992 | bytes 6891520 | tf_op jit(solution)/shard_map/dot_general | solution.py:22
  169.1 41.9 %all-to-all-done.1 = bf16[64,32,1344]{2,1,0:T(8,128)(2,1)} async-done(((bf16[64,32,1344]{2,1,0:T(8,128)(2,1)}), bf16[64,32,1344]{2,1,0:T(8,128)(2,1)}, u32[]{:S(2)}, u32[]{:S(2)}) %all-to-all-start.1) | async-done | bytes 5505056 | tf_op jit(solution)/shard_map/all_to_all | solution.py:215
  211.0 7.8 %fusion.79 = bf16[512,1344]{0,1:T(8,128)(2,1)S(1)} fusion(bf16[512,1344]{0,1:T(8,128)(2,1)} %fusion.73, bf16[2048,1344]{1,0:T(8,128)(2,1)} %bitcast.3, s32[2048]{0:T(1024)S(1)} %broadcast_add_fusion, s32[512]{0:T(512)S(1)} %get-tuple-element.48), kind=kOutput, calls=%fused_computation.81 | convolution fusion | flops 2820997120 | bytes 8267776 | tf_op jit(solution)/shard_map/dot_general | solution.py:22
  218.8 3.8 collective-permute-start.3
  222.6 5.8 %fusion.61 = bf16[512,1344]{0,1:T(8,128)(2,1)S(1)} fusion(bf16[2048,1344]{1,0:T(8,128)(2,1)} %bitcast.1, s32[2048]{0:T(1024)S(1)} %add.422, s32[512]{0:T(512)S(1)} %get-tuple-element.47), kind=kOutput, calls=%fused_computation.75 | convolution fusion | flops 2820308992 | bytes 6891520 | tf_op jit(solution)/shard_map/dot_general | solution.py:22
  228.9 5.8 %fusion.67 = bf16[512,1344]{0,1:T(8,128)(2,1)S(1)} fusion(bf16[2048,1344]{1,0:T(8,128)(2,1)} %bitcast.1, s32[2048]{0:T(1024)S(1)} %add.422, s32[512]{0:T(512)S(1)} %get-tuple-element.46), kind=kOutput, calls=%fused_computation.77 | convolution fusion | flops 2820308992 | bytes 6891520 | tf_op jit(solution)/shard_map/dot_general | solution.py:22
  234.8 16.8 %collective-permute-done.3 = bf16[512,1344]{0,1:T(8,128)(2,1)S(1)} collective-permute-done((bf16[512,1344]{0,1:T(8,128)(2,1)S(1)}, bf16[512,1344]{0,1:T(8,128)(2,1)S(1)}, u32[]{:S(2)}, u32[]{:S(2)}) %collective-permute-start.3) | collective-permute-done | bytes 1376288 | tf_op jit(solution)/shard_map/ppermute | solution.py:247
  251.6 6.3 %select_convert_fusion.1 = (f32[512,1344]{0,1:T(8,128)S(1)}, f32[512,1344]{0,1:T(8,128)S(1)}) fusion(bf16[512,1344]{0,1:T(8,128)(2,1)S(1)} %collective-permute-done.3, pred[512]{0:T(512)(128)(4,1)S(1)} %get-tuple-element.45, bf16[512,1344]{0,1:T(8,128)(2,1)S(1)} %fusion.67, bf16[2048,1344]{1,0:T(8,128)(2,1)} %bitcast.3, s32[2048]{0:T(1024)S(1)} %broadcast_add_fusion, ...), kind=kOutput, calls=%fused_computation.138 | convolution fusion | flops 2823749632 | bytes 13773312 | tf_op jit(solution)/shard_map/dot_general | solution.py:22
  259.6 21.5 %collective-permute-done.1 = bf16[512,1344]{0,1:T(8,128)(2,1)S(1)} collective-permute-done((bf16[512,1344]{0,1:T(8,128)(2,1)S(1)}, bf16[512,1344]{0,1:T(8,128)(2,1)S(1)}, u32[]{:S(2)}, u32[]{:S(2)}) %collective-permute-start.1) | collective-permute-done | bytes 1376288 | tf_op jit(solution)/shard_map/ppermute | solution.py:247
  281.0 6.2 %select_convert_fusion.3 = (f32[512,1344]{0,1:T(8,128)S(1)}, f32[512,1344]{0,1:T(8,128)S(1)}) fusion(bf16[512,1344]{0,1:T(8,128)(2,1)S(1)} %collective-permute-done.1, pred[512]{0:T(512)(128)(4,1)S(1)} %get-tuple-element.31, bf16[2048,1344]{1,0:T(8,128)(2,1)} %bitcast.1, s32[2048]{0:T(1024)S(1)} %add.422, s32[512]{0:T(512)S(1)} %get-tuple-element.32), kind=kOutput, calls=%fused_computation.140 | convolution fusion | flops 2823061504 | bytes 12397056 | tf_op jit(solution)/shard_map/dot_general | solution.py:22
  307.1 5.0 %fusion.120 = f32[1280,1344]{0,1:T(8,128)} fusion(bf16[512,576]{0,1:T(8,128)(2,1)S(1)} %get-tuple-element.55, bf16[512,768]{0,1:T(8,128)(2,1)S(1)} %get-tuple-element.53, bf16[512,1280]{1,0:T(8,128)(2,1)S(1)} %copy-done.5, f32[512]{0:T(512)S(1)} %add_rsqrt_fusion.1, f32[512]{0:T(512)S(1)} %broadcast_multiply_fusion.5), kind=kOutput, calls=%fused_computation.158 | convolution fusion | flops 1766981632 | bytes 9572352 | tf_op jit(solution)/shard_map/dot_general | solution.py:32
  312.1 4.2 fusion.159
  316.3 4.1 fusion.15
  320.4 6.4 %copy.31 = bf16[1280,1344]{1,0:T(8,128)(2,1)} copy(bf16[1280,1344]{0,1:T(8,128)(2,1)} %fusion.15) | data formatting | bytes 6881280 | tf_op jit(solution)/shard_map/convert.2
  326.8 6.9 %fusion.14 = bf16[1280,1344]{0,1:T(8,128)(2,1)} fusion(f32[1280,1344]{0,1:T(8,128)} %fusion.120, bf16[512,576]{0,1:T(8,128)(2,1)S(1)} %copy-done.22, bf16[512,768]{0,1:T(8,128)(2,1)S(1)} %copy-done.20, bf16[512,1280]{1,0:T(8,128)(2,1)S(1)} %copy-done.10, f32[512]{0:T(512)S(1)} %add_rsqrt_fusion, f32[512]{0:T(512)S(1)} %broadcast_multiply_fusion.2), kind=kOutput, calls=%fused_computation.20 | convolution fusion | flops 1770422272 | bytes 13012992 | tf_op jit(solution)/shard_map/dot_general | solution.py:32
  333.7 6.0 %copy.30 = bf16[1280,1344]{1,0:T(8,128)(2,1)} copy(bf16[1280,1344]{0,1:T(8,128)(2,1)} %fusion.14) | data formatting | bytes 6881280 | tf_op jit(solution)/shard_map/convert.5
  345.2 6.5 %pad_maximum_fusion.part_ref = bf16[2,4,4,2,48,1344]{5,4,3,2,1,0:T(8,128)(2,1)} fusion(bf16[1,4,4,2,48,1344]{5,4,3,2,1,0:T(8,128)(2,1)S(1)} %bitcast.30, bf16[1,4,4,2,48,1344]{5,4,3,2,1,0:T(8,128)(2,1)} %bitcast.31), kind=kLoop, calls=%fused_computation.9 | loop fusion | flops 4128768 | bytes 16515072 | tf_op jit(solution)/shard_map/stack | solution.py:272
  355.2 52.5 %shard_map.94 = f32[48,1344]{1,0:T(8,128)S(1)} custom-call(bf16[2,4,4,2,48,1344]{5,4,3,2,1,0:T(8,128)(2,1)S(1)} %copy-done), custom_call_target="tpu_custom_call" | custom-call | tf_op jit(solution)/shard_map/pallas_call | solution.py:161
  409.8 4.8 %convolution_convert_fusion.1 = bf16[2048,1280]{1,0:T(8,128)(2,1)S(1)} fusion(bf16[512,1280]{1,0:T(8,128)(2,1)} %fusion.88, s32[512]{0:T(512)S(1)} %iota_add_fusion.2, s32[2048]{0:T(1024)S(1)} %convert_reduce_fusion), kind=kOutput, calls=%fused_computation.17 | convolution fusion | flops 2688024576 | bytes 6563840 | tf_op jit(solution)/shard_map/dot_general | solution.py:22
  417.9 4.6 %convolution_convert_fusion = bf16[2048,1280]{1,0:T(8,128)(2,1)S(1)} fusion(bf16[512,1280]{1,0:T(8,128)(2,1)} %collective-permute-done.4, s32[512]{0:T(512)S(1)} %copy-done.25, s32[2048]{0:T(1024)S(1)} %convert_reduce_fusion), kind=kOutput, calls=%fused_computation.16 | convolution fusion | flops 2688024576 | bytes 6563840 | tf_op jit(solution)/shard_map/dot_general | solution.py:22
  422.5 17.2 %collective-permute-done.2 = bf16[512,1280]{1,0:T(8,128)(2,1)S(1)} collective-permute-done((bf16[512,1280]{1,0:T(8,128)(2,1)S(1)}, bf16[512,1280]{1,0:T(8,128)(2,1)S(1)}, u32[]{:S(2)}, u32[]{:S(2)}) %collective-permute-start.2) | collective-permute-done | bytes 1310752 | tf_op jit(solution)/shard_map/ppermute | solution.py:267
  439.7 5.0 %fusion.18 = bf16[2048,1280]{1,0:T(8,128)(2,1)} fusion(bf16[2048,1280]{1,0:T(8,128)(2,1)S(1)} %convolution_convert_fusion, bf16[2048,1280]{1,0:T(8,128)(2,1)S(1)} %convolution_convert_fusion.1, bf16[2048,1280]{1,0:T(8,128)(2,1)S(1)} %convolution_convert_fusion.3, bf16[512,1280]{1,0:T(8,128)(2,1)S(1)} %collective-permute-done.2, s32[512]{0:T(512)S(1)} %copy-done.24, ...), kind=kOutput, calls=%fused_computation.24 | convolution fusion | flops 2695888896 | bytes 22292480 | tf_op jit(solution)/shard_map/dot_general | solution.py:22
  (116 shorter events, 68.5 us)
Async XLA Ops:
  0.6 2.8 copy-start.16
  3.5 2.4 copy-start.1
  5.9 5.3 %copy-start.26 = (s32[2048]{0:T(1024)S(1)}, s32[2048]{0:T(1024)}, u32[]{:S(2)}) copy-start(s32[2048]{0:T(1024)} %param.12) | copy-start | bytes 24580
  5.9 136.2 %collective-permute-start = (bf16[1280,1344]{0,1:T(8,128)(2,1)}, bf16[1280,1344]{0,1:T(8,128)(2,1)}, u32[]{:S(2)}, u32[]{:S(2)}) collective-permute-start(bf16[1280,1344]{0,1:T(8,128)(2,1)} %pad_maximum_fusion.4), channel_id=1, source_target_pairs={{0,64},{64,0},{1,65},{65,1},{2,66},{66,2},{3,67},{67,3},{4,68},{68... | collective-permute-start | bytes 10321928 | tf_op jit(solution)/shard_map/ppermute | solution.py:203
  35.4 80.9 %all-to-all-start = ((bf16[64,32,1344]{2,1,0:T(8,128)(2,1)}), bf16[64,32,1344]{2,1,0:T(8,128)(2,1)}, u32[]{:S(2)}, u32[]{:S(2)}) async-start(bf16[64,32,1344]{2,1,0:T(8,128)(2,1)} %bitcast.28), calls=%async_computation | async-start | bytes 11534336 | tf_op jit(solution)/shard_map/all_to_all | solution.py:215
  63.0 9.8 %copy-start.23 = (s32[2048]{0:T(1024)S(1)}, s32[2048]{0:T(1024)}, u32[]{:S(2)}) copy-start(s32[2048]{0:T(1024)} %param.13) | copy-start | bytes 24580
  89.0 52.5 %copy-start.3 = (bf16[512,1280]{1,0:T(8,128)(2,1)}, bf16[512,1280]{1,0:T(8,128)(2,1)S(1)}, u32[]{:S(2)}) copy-start(bf16[512,1280]{1,0:T(8,128)(2,1)S(1)} %get-tuple-element.65) | copy-start | bytes 3932164
  116.3 94.7 %all-to-all-start.1 = ((bf16[64,32,1344]{2,1,0:T(8,128)(2,1)}), bf16[64,32,1344]{2,1,0:T(8,128)(2,1)}, u32[]{:S(2)}, u32[]{:S(2)}) async-start(bf16[64,32,1344]{2,1,0:T(8,128)(2,1)} %bitcast.29), calls=%async_computation.1 | async-start | bytes 11534336 | tf_op jit(solution)/shard_map/all_to_all | solution.py:215
  142.0 3.8 copy-start.8
  145.8 11.2 %copy-start.17 = (bf16[1280,1344]{0,1:T(8,128)(2,1)}, bf16[1280,1344]{0,1:T(8,128)(2,1)S(1)}, u32[]{:S(2)}) copy-start(bf16[1280,1344]{0,1:T(8,128)(2,1)S(1)} %get-tuple-element.36) | copy-start | bytes 10321924
  149.6 3.8 copy-start.4
  218.8 32.8 %collective-permute-start.3 = (bf16[512,1344]{0,1:T(8,128)(2,1)S(1)}, bf16[512,1344]{0,1:T(8,128)(2,1)S(1)}, u32[]{:S(2)}, u32[]{:S(2)}) collective-permute-start(bf16[512,1344]{0,1:T(8,128)(2,1)S(1)} %fusion.79), channel_id=1, source_target_pairs={{0,64},{64,0},{1,65},{65,1},{2,66},{66,2},{3,67},{67,3},{4,68},{68... | collective-permute-start | bytes 4128776 | tf_op jit(solution)/shard_map/ppermute | solution.py:247
  228.4 52.6 %collective-permute-start.1 = (bf16[512,1344]{0,1:T(8,128)(2,1)S(1)}, bf16[512,1344]{0,1:T(8,128)(2,1)S(1)}, u32[]{:S(2)}, u32[]{:S(2)}) collective-permute-start(bf16[512,1344]{0,1:T(8,128)(2,1)S(1)} %fusion.61), channel_id=1, source_target_pairs={{0,64},{64,0},{1,65},{65,1},{2,66},{66,2},{3,67},{67,3},{4,68},{68... | collective-permute-start | bytes 4128776 | tf_op jit(solution)/shard_map/ppermute | solution.py:247
  251.5 6.4 %copy-start.11 = (f32[512,1344]{0,1:T(8,128)S(1)}, f32[512,1344]{0,1:T(8,128)}, u32[]{:S(2)}) copy-start(f32[512,1344]{0,1:T(8,128)} %fusion.151) | copy-start | bytes 8257540
  251.5 6.7 %copy-start.12 = (f32[512,1344]{0,1:T(8,128)S(1)}, f32[512,1344]{0,1:T(8,128)}, u32[]{:S(2)}) copy-start(f32[512,1344]{0,1:T(8,128)} %fusion.149) | copy-start | bytes 8257540
  281.0 6.2 %copy-start.13 = (f32[512,1344]{0,1:T(8,128)S(1)}, f32[512,1344]{0,1:T(8,128)}, u32[]{:S(2)}) copy-start(f32[512,1344]{0,1:T(8,128)} %fusion.157) | copy-start | bytes 8257540
  290.5 2.0 copy-start.18
  292.5 2.3 copy-start.5
  297.7 3.3 copy-start.21
  298.6 2.3 copy-start.19
  298.6 2.3 copy-start.9
  305.9 112.0 %collective-permute-start.4 = (bf16[512,1280]{1,0:T(8,128)(2,1)}, bf16[512,1280]{1,0:T(8,128)(2,1)}, u32[]{:S(2)}, u32[]{:S(2)}) collective-permute-start(bf16[512,1280]{1,0:T(8,128)(2,1)} %fusion.88), channel_id=1, source_target_pairs={{0,64},{64,0},{1,65},{65,1},{2,66},{66,2},{3,67},{67,3},{4,68},{68... | collective-permute-start | bytes 3932168 | tf_op jit(solution)/shard_map/ppermute | solution.py:267
  320.4 6.4 %copy-start.10 = (bf16[512,1280]{1,0:T(8,128)(2,1)S(1)}, bf16[512,1280]{1,0:T(8,128)(2,1)}, u32[]{:S(2)}) copy-start(bf16[512,1280]{1,0:T(8,128)(2,1)} %copy-done.7) | copy-start | bytes 3932164
  320.4 6.4 %copy-start.20 = (bf16[512,768]{0,1:T(8,128)(2,1)S(1)}, bf16[512,768]{0,1:T(8,128)(2,1)}, u32[]{:S(2)}) copy-start(bf16[512,768]{0,1:T(8,128)(2,1)} %copy-done.19) | copy-start | bytes 2359300
  320.4 6.4 %copy-start.22 = (bf16[512,576]{0,1:T(8,128)(2,1)S(1)}, bf16[512,576]{0,1:T(8,128)(2,1)}, u32[]{:S(2)}) copy-start(bf16[512,576]{0,1:T(8,128)(2,1)} %copy-done.21) | copy-start | bytes 1769476
  339.7 3.1 copy-start.2
  351.7 3.5 copy-start
  355.2 52.5 %copy-start.6 = (bf16[512,1280]{1,0:T(8,128)(2,1)S(1)}, bf16[512,1280]{1,0:T(8,128)(2,1)}, u32[]{:S(2)}) copy-start(bf16[512,1280]{1,0:T(8,128)(2,1)} %copy-done.3) | copy-start | bytes 3932164
  355.2 52.5 %copy-start.15 = (f32[512,1280]{1,0:T(8,128)S(1)}, f32[512,1280]{1,0:T(8,128)}, u32[]{:S(2)}) copy-start(f32[512,1280]{1,0:T(8,128)} %get-tuple-element.66) | copy-start | bytes 7864324
  409.8 29.9 %collective-permute-start.2 = (bf16[512,1280]{1,0:T(8,128)(2,1)S(1)}, bf16[512,1280]{1,0:T(8,128)(2,1)S(1)}, u32[]{:S(2)}, u32[]{:S(2)}) collective-permute-start(bf16[512,1280]{1,0:T(8,128)(2,1)S(1)} %fusion.93), channel_id=1, source_target_pairs={{0,64},{64,0},{1,65},{65,1},{2,66},{66,2},{3,67},{67,3},{4,68},{68... | collective-permute-start | bytes 3932168 | tf_op jit(solution)/shard_map/ppermute | solution.py:267
  414.6 3.3 copy-start.25
  417.9 21.8 %copy-start.24 = (s32[512]{0:T(512)S(1)}, s32[512]{0:T(512)}, u32[]{:S(2)}) copy-start(s32[512]{0:T(512)} %iota_add_fusion.3) | copy-start | bytes 6148
  (2 other events, 2.8 us)

commit v2 on v1

v2 whole, which is shorter than its diff:
```python
import functools
import math

import jax
import jax.numpy as jnp
from jax import lax
from jax.experimental import pallas as pl
from jax.experimental.pallas import tpu as pltpu
from jax.sharding import PartitionSpec as P

E1 = 1536
E2 = 1152
CHUNKS = ((0, 32), (32, 32))
TILE = 256

norm_eps = 1e-05
length_eps = 1e-06
MESH = pl.DeviceIdType.MESH
BF = jnp.bfloat16
F32 = jnp.float32
I32 = jnp.int32
HERE = pl.BlockSpec(memory_space=pl.ANY)
VMEM = pl.BlockSpec(memory_space=pltpu.VMEM)


def tile_of(rows):
    return next(size for size in (512, 384, 256, 128, 64, 32, 16) if rows % size == 0)


def whole(shape):
    return pl.BlockSpec(shape, lambda i: (0,) * len(shape), pipeline_mode=pl.Buffered(1))


def tiles(rows, width, first=0):
    return pl.BlockSpec((rows, width), lambda i: (first // rows + i, 0))


def local_call(kernel, steps, in_specs, out_specs, out_shape, *operands):
    return pl.pallas_call(
        kernel,
        grid=(steps,),
        in_specs=in_specs,
        out_specs=out_specs,
        out_shape=out_shape,
        compiler_params=pltpu.CompilerParams(vmem_limit_bytes=56 * 2**20),
        cost_estimate=pl.CostEstimate(flops=2**20, bytes_accessed=2**16, transcendentals=0),
    )(*operands)


def hits(column, first, count):
    return (column == first + lax.broadcasted_iota(I32, (column.shape[0], count), 1)).astype(BF)


def back_product(left_op, right_op):
    return lax.dot_general(
        left_op, right_op, (((1,), (1,)), ((), ())), preferred_element_type=F32
    )


def outbox_kernel(place_ref, dino_ref, siglip_ref, after_ref, out_ref):
    rows, count = out_ref.shape[0], dino_ref.shape[0]
    cols = dino_ref.shape[1]
    row = pl.program_id(0) * rows + lax.broadcasted_iota(I32, (rows, count), 0)
    hit = (row == place_ref[...]).astype(BF)
    out_ref[:, :cols] = jnp.dot(hit, dino_ref[...], preferred_element_type=F32).astype(BF)
    out_ref[:, cols:] = back_product(hit, siglip_ref[...]).astype(BF)


def fill_outbox(place, dino_feat, siglip_feat, rows, after):
    width = dino_feat.shape[1] + siglip_feat.shape[0]
    tile = tile_of(rows)
    return local_call(
        outbox_kernel, rows // tile,
        [whole((1, place.shape[1])), whole(dino_feat.shape), whole(siglip_feat.shape), HERE],
        tiles(tile, width), jax.ShapeDtypeStruct((rows, width), BF),
        place, dino_feat, siglip_feat, after)


def greet(devices):
    barrier = pltpu.get_barrier_semaphore()
    for device in devices:
        pl.semaphore_signal(barrier, inc=1, device_id=device, device_id_type=MESH)
    pl.semaphore_wait(barrier, len(devices))


def tile_at(i, start=0):
    return pl.ds(pl.multiple_of(start + i * TILE, TILE), TILE)


def remote(src, dst, send_sem, recv_sem, device):
    return pltpu.make_async_remote_copy(
        src_ref=src, dst_ref=dst, send_sem=send_sem, recv_sem=recv_sem, device_id=device, device_id_type=MESH)


def forward_kernel(columns_ref, rank_ref, place_ref, student_ref, dino_feat_ref, siglip_feat_ref, dino_ref, siglip_ref,
                   after_ref, normed_ref, bf_ref, inv_ref, out_ref, out_far_ref, dino_far_ref, siglip_far_ref,
                   outbox_ref, send_sem, recv_sem):
    dp, t = lax.axis_index("dp"), lax.axis_index("tsec")
    core = dp % 2
    partner, sibling = {"tsec": 1 - t}, {"dp": dp + 1 - 2 * core}
    greet([partner, sibling])
    cols = dino_ref.shape[1]

    fetches, swaps = [], []
    for i, (own, far) in enumerate(((dino_ref, dino_far_ref), (siglip_ref, siglip_far_ref))):
        size = own.shape[0] // 2
        part = pl.ds(pl.multiple_of(core * size, 16), size)
        fetches.append(remote(own.at[part], far.at[part], send_sem.at[i], recv_sem.at[i], partner))
        swaps.append(remote(far.at[part], far.at[part], send_sem.at[2 + i], recv_sem.at[2 + i], sibling))
    for copy in fetches:
        copy.start()

    @pl.loop(0, outbox_ref.shape[0] // TILE)
    def _(i):
        count = dino_feat_ref.shape[0]
        row = i * TILE + lax.broadcasted_iota(I32, (TILE, count), 0)
        hit = (row == place_ref[...]).astype(BF)
        outbox_ref[tile_at(i), :cols] = jnp.dot(hit, dino_feat_ref[...], preferred_element_type=F32).astype(BF)
        outbox_ref[tile_at(i), cols:] = back_product(hit, siglip_feat_ref[...]).astype(BF)

    @pl.loop(0, out_ref.shape[0] // TILE)
    def _(i):
        hit = (columns_ref[tile_at(i), 0:1] == rank_ref[...]).astype(BF)
        rows = jnp.dot(hit, student_ref[...], preferred_element_type=F32)
        centred = rows - jnp.mean(rows, 1, keepdims=True)
        inv_dev = lax.rsqrt(jnp.mean(centred * centred, 1, keepdims=True) + norm_eps)
        normed = centred * inv_dev
        normed_bf = normed.astype(BF)
        normed_ref[tile_at(i)] = normed
        bf_ref[tile_at(i)] = normed_bf
        inv_ref[tile_at(i)] = inv_dev
        out_ref[tile_at(i), :cols] = jnp.dot(normed_bf, dino_ref[...], preferred_element_type=F32)
        out_ref[tile_at(i), cols:] = back_product(normed_bf, siglip_ref[...])

    for copy, swap in zip(fetches, swaps):
        copy.wait_recv()
        swap.start()
    for swap in swaps:
        swap.wait_recv()

    @pl.loop(0, out_ref.shape[0] // TILE)
    def _(i):
        normed_bf = bf_ref[tile_at(i)]
        out_far_ref[tile_at(i), :cols] = jnp.dot(normed_bf, dino_far_ref[...], preferred_element_type=F32)
        out_far_ref[tile_at(i), cols:] = back_product(normed_bf, siglip_far_ref[...])

    for copy in fetches + swaps:
        copy.wait_send()


def forward(columns, rank, place, student, dino_feat, siglip_feat, weights, rows_out, after):
    rows, features = columns.shape[0], student.shape[1]
    width = weights[0].shape[1] + weights[1].shape[0]
    return pl.pallas_call(
        forward_kernel,
        in_specs=[VMEM] * 8 + [HERE],
        out_specs=[VMEM] * 8,
        out_shape=[
            jax.ShapeDtypeStruct((rows, features), F32), jax.ShapeDtypeStruct((rows, features), BF),
            jax.ShapeDtypeStruct((rows, 1), F32), jax.ShapeDtypeStruct((rows, width), F32),
            jax.ShapeDtypeStruct((rows, width), F32), jax.ShapeDtypeStruct(weights[0].shape, BF),
            jax.ShapeDtypeStruct(weights[1].shape, BF), jax.ShapeDtypeStruct((rows_out, width), BF)],
        scratch_shapes=[pltpu.SemaphoreType.DMA((4,)), pltpu.SemaphoreType.DMA((4,))],
        compiler_params=pltpu.CompilerParams(
            collective_id=1, has_side_effects=True, vmem_limit_bytes=60 * 2**20),
        cost_estimate=pl.CostEstimate(flops=3 * 10**10, bytes_accessed=5 * 10**7, transcendentals=0),
    )(columns, rank, place, student, dino_feat, siglip_feat, *weights, after)


def head_delta(outputs, targets, head_width):
    out_sq = sum(jnp.sum(y * y, 1, keepdims=True) for y in outputs)
    tgt_sq = sum(jnp.sum(f * f, 1, keepdims=True) for f in targets)
    cross = sum(jnp.sum(y * f, 1, keepdims=True) for y, f in zip(outputs, targets))
    out_len = jnp.sqrt(out_sq + length_eps)
    tgt_len = jnp.sqrt(tgt_sq + length_eps)
    cosine = cross / (out_len * tgt_len)
    pull_f = head_width / (out_len * tgt_len)
    pull_y = head_width * cosine / (out_len * out_len)
    return [
        (jnp.clip(y - f, -1.0, 1.0) - (pull_f * f - pull_y * y)).astype(BF)
        for y, f in zip(outputs, targets)
    ]


def block_kernel(stage, columns_ref, columns_far_ref, inv_ref, inbox_ref, out_ref, out_far_ref, normed_ref,
                 dino_ref, siglip_ref, dino_far_ref, siglip_far_ref, *refs):
    if stage == 0:
        delta_ref, delta_far_ref, grad_ref, base_far_ref, base_ref = refs[:5]
        refs = refs[5:]
    else:
        base_far_ref, base_ref, _, delta_ref, delta_far_ref, grad_ref = refs[:6]
        refs = refs[6:]
    table, out, out_far, normed_all, dino_w, siglip_w, dino_far_w, siglip_far_w, sent, came, near_all = refs[:11]
    copy_sem, send_sem, recv_sem = refs[11:]
    rows = delta_ref.shape[0]
    first = stage * rows
    cols = dino_w.shape[1]
    loads = [
        pltpu.make_async_copy(src, dst, copy_sem.at[i])
        for i, (src, dst) in enumerate((
            (inbox_ref, table), (dino_ref, dino_w), (siglip_ref, siglip_w), (dino_far_ref, dino_far_w),
            (siglip_far_ref, siglip_far_w), (out_ref.at[pl.ds(first, rows)], out),
            (out_far_ref.at[pl.ds(first, rows)], out_far), (normed_ref.at[pl.ds(first, rows)], normed_all)))
    ]
    for load in loads:
        load.start()
    partner = {"tsec": 1 - lax.axis_index("tsec")}
    greet([partner])

    def swap(i):
        return remote(sent.at[tile_at(i)], came.at[tile_at(i)], send_sem.at[i], recv_sem.at[i], partner)

    def look_up(column):
        hit = (column == lax.broadcasted_iota(I32, (TILE, table.shape[0]), 1)).astype(BF)
        return jnp.dot(hit, table[...], preferred_element_type=F32)

    loads[0].wait()
    steps = rows // TILE
    for i in range(steps):
        found = look_up(columns_far_ref[tile_at(i, first), 2 + stage : 3 + stage])
        if stage:
            found = found + base_far_ref[tile_at(i)].astype(F32)
        sent[tile_at(i)] = found.astype(BF)
        swap(i).start()
    for i in range(steps):
        found = look_up(columns_ref[tile_at(i, first), 2 + stage : 3 + stage])
        if stage:
            found = found + base_ref[tile_at(i)].astype(F32)
        near_all[tile_at(i)] = found.astype(BF)
    if stage == 0:
        for i in range(steps):
            base_far_ref[tile_at(i)] = look_up(columns_far_ref[tile_at(i, rows), 2:3]).astype(BF)
            base_ref[tile_at(i)] = look_up(columns_ref[tile_at(i, rows), 2:3]).astype(BF)
    for load in loads[1:]:
        load.wait()
    for i in range(steps):
        swap(i).wait_recv()
        near, far = near_all[tile_at(i)].astype(F32), came[tile_at(i)].astype(F32)
        direct = columns_ref[tile_at(i, first), 1:2] > 0
        own = jnp.where(direct, near, far)
        other = jnp.where(direct, far, near)
        y, y_far = out[tile_at(i)], out_far[tile_at(i)]
        dino = head_delta([y[:, :cols], y_far[:, :cols]], [own[:, :cols], other[:, :cols]], float(E1))
        siglip = head_delta([y[:, cols:], y_far[:, cols:]], [own[:, cols:], other[:, cols:]], float(E2))
        for delta, d, g in ((delta_ref, dino[0], siglip[0]), (delta_far_ref, dino[1], siglip[1])):
            delta[tile_at(i), :cols] = d
            delta[tile_at(i), cols:] = g
        part = back_product(dino[0], dino_w[...]) + jnp.dot(siglip[0], siglip_w[...], preferred_element_type=F32)
        part_far = back_product(dino[1], dino_far_w[...]) + jnp.dot(
            siglip[1], siglip_far_w[...], preferred_element_type=F32)
        normed_grad = part.astype(BF).astype(F32) + part_far.astype(BF).astype(F32)
        normed = normed_all[tile_at(i)]
        grad_mean = jnp.mean(normed_grad, 1, keepdims=True)
        grad_proj = jnp.mean(normed_grad * normed, 1, keepdims=True)
        inv_dev = inv_ref[tile_at(i, first)]
        grad_ref[tile_at(i)] = ((normed_grad - grad_mean - normed * grad_proj) * inv_dev).astype(BF)
    for i in range(steps):
        swap(i).wait_send()


def handle_block(stage, columns, columns_far, inv_dev, inbox, out, out_far, normed, weights, bases):
    rows, features = normed.shape[0] // 2, normed.shape[1]
    width = inbox.shape[1]
    wide, thin = jax.ShapeDtypeStruct((rows, width), BF), jax.ShapeDtypeStruct((rows, features), BF)
    shapes = [wide, wide, thin] + ([wide, wide] if stage == 0 else [])
    return pl.pallas_call(
        functools.partial(block_kernel, stage),
        in_specs=[VMEM] * 3 + [HERE] * 8 + ([VMEM, VMEM, HERE] if stage else []),
        out_specs=[VMEM] * len(shapes),
        out_shape=shapes,
        scratch_shapes=[
            pltpu.VMEM(inbox.shape, BF), pltpu.VMEM((rows, width), F32), pltpu.VMEM((rows, width), F32),
            pltpu.VMEM((rows, features), F32)] + [pltpu.VMEM(w.shape, BF) for w in weights] + [
            pltpu.VMEM((rows, width), BF), pltpu.VMEM((rows, width), BF), pltpu.VMEM((rows, width), BF),
            pltpu.SemaphoreType.DMA((8,)), pltpu.SemaphoreType.DMA((rows // TILE,)),
            pltpu.SemaphoreType.DMA((rows // TILE,))],
        compiler_params=pltpu.CompilerParams(
            collective_id=2 + stage, has_side_effects=True, vmem_limit_bytes=60 * 2**20),
        cost_estimate=pl.CostEstimate(flops=10**10, bytes_accessed=3 * 10**7, transcendentals=0),
    )(columns, columns_far, inv_dev, inbox, out, out_far, normed, *weights, *bases)


def wgrad_kernel(n, bf_ref, *refs):
    deltas, base, part_ref = refs[:n], refs[n:-1], refs[-1]
    blocks, rows = part_ref.shape[1], bf_ref.shape[1] // part_ref.shape[1]
    for side in (0, 1):
        total, start = 0.0, 0
        for delta in deltas[side::2]:
            size = delta.shape[0]
            total = total + lax.dot_general(
                bf_ref[start : start + size], delta[...], (((0,), (0,)), ((), ())), preferred_element_type=F32)
            start += size
        for b in range(blocks):
            value = total[b * rows : (b + 1) * rows]
            if base:
                value = value + base[0][side, b, :rows].astype(F32)
            part_ref[side, b, :rows] = value.astype(BF)
            part_ref[side, b, rows:] = jnp.zeros((part_ref.shape[2] - rows, part_ref.shape[3]), BF)


def wgrad_part(normed_bf, deltas, first, owners, padded, base=None):
    features = normed_bf.shape[1]
    rows = sum(d.shape[0] for d in deltas[::2])
    width = deltas[0].shape[1]
    split = 2
    blocks = pl.BlockSpec((2, owners // split, padded, width), lambda i: (0, i, 0, 0))
    more = [] if base is None else [base]
    return pl.pallas_call(
        functools.partial(wgrad_kernel, len(deltas)),
        grid=(split,),
        in_specs=[pl.BlockSpec((rows, features // split), lambda i: (first // rows, i))]
        + [whole(d.shape) for d in deltas] + [blocks for _ in more],
        out_specs=blocks,
        out_shape=jax.ShapeDtypeStruct((2, owners, padded, width), BF),
        compiler_params=pltpu.CompilerParams(vmem_limit_bytes=58 * 2**20),
        cost_estimate=pl.CostEstimate(flops=2**20, bytes_accessed=2**16, transcendentals=0),
    )(normed_bf, *deltas, *more)


def unpick_kernel(n, rank_ref, starts_ref, *refs):
    pieces, base, out_ref = refs[:n], refs[n:-1], refs[-1]
    total = base[0][...].astype(F32) if base else 0.0
    for i, piece in enumerate(pieces):
        hit = hits(rank_ref[...], starts_ref[i], piece.shape[0])
        total = total + jnp.dot(hit, piece[...], preferred_element_type=F32)
    out_ref[...] = total.astype(BF)


def unpick(rank, starts, pieces, base=None):
    rows, width = rank.shape[0], pieces[0].shape[1]
    more = [] if base is None else [base]
    tile = tile_of(rows)
    return local_call(
        lambda *refs: unpick_kernel(len(pieces), *refs), rows // tile,
        [tiles(tile, 1), pl.BlockSpec(memory_space=pltpu.SMEM)] + [whole(p.shape) for p in pieces]
        + [tiles(tile, width) for _ in more],
        tiles(tile, width), jax.ShapeDtypeStruct((rows, width), BF),
        rank, starts, *pieces, *more)


def place():
    dp = lax.axis_index("dp")
    x = lax.axis_index("rep") * 2 + lax.axis_index("tsec")
    return x, dp // 8, (dp // 2) % 4, dp % 2


def at_place(x, y, z, c):
    return {"tsec": x % 2, "dp": (y * 4 + z) * 2 + c, "rep": x // 2}


def sum_kernel(part_ref, out_ref, held, pair, far_y, far_z, far_y2, far_z2, far_x, stage,
               own_sem, pair_send, pair_recv, send_sem, recv_sem):
    x, y, z, c = place()
    t = x % 2
    lines = [[at_place(x, (y + j) % 4, z, c), at_place(x, y, (z + j) % 4, c), at_place((x + j) % 4, y, z, c)]
             for j in (1, 2, 3)]
    greet([at_place(x, y, z, 1 - c)] + sum(lines, []))

    order = (2, 1, 3, 0)

    def pair_copy(k, j, i):
        line = (y + j) % 4 if k == 0 else (z + j) % 4
        src = part_ref.at[t, line, :, 1 - c] if k == 0 else part_ref.at[1 - t, :, line, 1 - c]
        return pltpu.make_async_remote_copy(
            src_ref=src, dst_ref=pair.at[k, j], send_sem=pair_send.at[i], recv_sem=pair_recv.at[i],
            device_id=at_place(x, y, z, 1 - c), device_id_type=MESH)

    def own_copy(k, j, i):
        line = (y + j) % 4 if k == 0 else (z + j) % 4
        src = part_ref.at[t, line, :, c] if k == 0 else part_ref.at[1 - t, :, line, c]
        return pltpu.make_async_copy(src, held.at[k, j], own_sem.at[i])

    def line_copy(k, j, i):
        far = far_y if k == 0 else far_z
        device = at_place(x, (y + j) % 4, z, c) if k == 0 else at_place(x, y, (z + j) % 4, c)
        return pltpu.make_async_remote_copy(
            src_ref=held.at[k, j], dst_ref=far.at[j - 1], send_sem=send_sem.at[i], recv_sem=recv_sem.at[i],
            device_id=device, device_id_type=MESH)

    steps = [(k, j) for j in order for k in (0, 1)]
    for i, (k, j) in enumerate(steps):
        pair_copy(k, j, i).start()
        own_copy(k, j, i).start()
    for i, (k, j) in enumerate(steps):
        own_copy(k, j, i).wait()
        pair_copy(k, j, i).wait_recv()

        @pl.loop(0, 4)
        def _(b, k=k, j=j):
            held[k, j, b] = (held[k, j, b].astype(F32) + pair[k, j, b].astype(F32)).astype(BF)

        if j:
            line_copy(k, j, k * 3 + j - 1).start()
    for i, (k, j) in enumerate(steps):
        pair_copy(k, j, i).wait_send()
    for k in (0, 1):
        for j in (2, 1, 3):
            line_copy(k, j, k * 3 + j - 1).wait()
        far = far_y if k == 0 else far_z

        @pl.loop(0, 4)
        def _(b, k=k, far=far):
            held[k, 0, b] = (held[k, 0, b].astype(F32) + far[0, b].astype(F32)
                             + far[1, b].astype(F32) + far[2, b].astype(F32)).astype(BF)

    def cross_copy(k, j):
        far = far_z2 if k == 0 else far_y2
        b = (z + j) % 4 if k == 0 else (y + j) % 4
        device = at_place(x, y, b, c) if k == 0 else at_place(x, b, z, c)
        i = 6 + k * 3 + j - 1
        return pltpu.make_async_remote_copy(
            src_ref=held.at[k, 0, b], dst_ref=far.at[j - 1], send_sem=send_sem.at[i], recv_sem=recv_sem.at[i],
            device_id=device, device_id_type=MESH)

    for k in (0, 1):
        for j in (2, 1, 3):
            cross_copy(k, j).start()
    for k in (0, 1):
        for j in (2, 1, 3):
            cross_copy(k, j).wait()
        far = far_z2 if k == 0 else far_y2
        mine = held[k, 0, z] if k == 0 else held[k, 0, y]
        stage[k] = (mine.astype(F32) + far[0].astype(F32) + far[1].astype(F32) + far[2].astype(F32)).astype(BF)

    def x_copy(j):
        device = (x + j) % 4
        i = 12 + j - 1
        return pltpu.make_async_remote_copy(
            src_ref=stage.at[device % 2], dst_ref=far_x.at[j - 1], send_sem=send_sem.at[i], recv_sem=recv_sem.at[i],
            device_id=at_place(device, y, z, c), device_id_type=MESH)

    for j in (2, 1, 3):
        x_copy(j).start()
    for j in (2, 1, 3):
        x_copy(j).wait()
    out_ref[...] = (stage[t].astype(F32) + far_x[0].astype(F32) + far_x[1].astype(F32) + far_x[2].astype(F32))


def sum_parts(part):
    rows, width = part.shape[-2:]
    block = (rows, width)
    return pl.pallas_call(
        sum_kernel,
        out_shape=jax.ShapeDtypeStruct(block, F32),
        in_specs=[pl.BlockSpec(memory_space=pl.ANY)],
        out_specs=pl.BlockSpec(memory_space=pltpu.VMEM),
        scratch_shapes=[
            pltpu.VMEM((2, 4, 4) + block, BF),
            pltpu.VMEM((2, 4, 4) + block, BF),
            pltpu.VMEM((3, 4) + block, BF),
            pltpu.VMEM((3, 4) + block, BF),
            pltpu.VMEM((3,) + block, BF),
            pltpu.VMEM((3,) + block, BF),
            pltpu.VMEM((3,) + block, BF),
            pltpu.VMEM((2,) + block, BF),
            pltpu.SemaphoreType.DMA((8,)),
            pltpu.SemaphoreType.DMA((8,)),
            pltpu.SemaphoreType.DMA((8,)),
            pltpu.SemaphoreType.DMA((15,)),
            pltpu.SemaphoreType.DMA((15,)),
        ],
        compiler_params=pltpu.CompilerParams(
            collective_id=0, has_side_effects=True, vmem_limit_bytes=58 * 2**20
        ),
    )(part)


def per_device(student, dino_feat, siglip_feat, dino_weight, siglip_weight, send_index, recv_index):
    n_dp = lax.axis_size("dp")
    groups = n_dp * lax.axis_size("rep")
    row_count = student.shape[0]
    capacity = 2 * row_count // groups
    dino_cols = dino_feat.shape[1]
    t = lax.axis_index("tsec")
    rep = lax.axis_index("rep")
    swap = [(0, 1), (1, 0)]
    mirrored = [
        [((tt ^ r) * n_dp + d) * 2 + r for d in range(n_dp) for r in range(2)] for tt in range(2)
    ]

    own_rows = student.shape[1] // n_dp
    padded = -(-own_rows // 16) * 16

    def place_in(chunk, code):
        start, size = CHUNKS[chunk]
        slot = code % capacity - start
        return jnp.where((slot >= 0) & (slot < size), code // capacity * size + slot, -1)

    def exchange(outbox, chunk):
        arrived = lax.all_to_all(
            outbox.reshape(groups, CHUNKS[chunk][1], -1),
            ("tsec", "dp", "rep"),
            split_axis=0,
            concat_axis=0,
            axis_index_groups=mirrored,
            tiled=True,
        )
        return arrived.reshape(outbox.shape)

    outbox = fill_outbox(
        place_in(0, send_index)[None, :], dino_feat, siglip_feat.T, groups * CHUNKS[0][1], send_index)
    inbox = exchange(outbox, 0)

    key = (recv_index % capacity) * groups + recv_index // capacity
    rank = jnp.sum((key[:, None] > key[None, :]).astype(I32), 1)
    ranks = jnp.arange(row_count, dtype=I32)
    code_at = jnp.sum(jnp.where(rank[None, :] == ranks[:, None], recv_index[None, :], 0), 1)
    quarter = row_count // 4

    def columns_of(whose):
        codes, order = [
            jnp.concatenate([
                lax.dynamic_slice(values, ((2 * stage + whose) * quarter,), (quarter,)) for stage in (0, 1)
            ])
            for values in (code_at, ranks)
        ]
        direct = ((codes // capacity) % 2 == rep).astype(I32)
        return jnp.stack([order, direct] + [place_in(c, codes) for c in range(len(CHUNKS))], 1)

    columns, columns_far = columns_of(t), columns_of(1 - t)
    weights = [dino_weight, siglip_weight.T]
    normed, normed_bf, inv_dev, out, out_far, *weights_far, outbox = forward(
        columns, rank[None, :], place_in(1, send_index)[None, :], student, dino_feat, siglip_feat.T, weights,
        groups * CHUNKS[1][1], outbox)
    weights = weights + weights_far
    inboxes = [inbox, exchange(outbox, 1)]

    part, bases, pieces, starts = None, [], [], []
    for stage in (0, 1):
        delta, delta_far, grad, *bases = handle_block(
            stage, columns, columns_far, inv_dev, inboxes[stage], out, out_far, normed, weights, bases)
        pieces += [grad, lax.ppermute(grad, "tsec", swap)]
        starts += [(2 * stage + t) * quarter, (2 * stage + 1 - t) * quarter]
        part = wgrad_part(normed_bf, [delta, delta_far], stage * quarter, n_dp, padded, part)
        bases = bases + [part]

    part = part.reshape((2, 4, 4, 2) + part.shape[2:])
    grad_scale = 1.0 / math.sqrt(row_count * groups)
    weight_grad = sum_parts(part)[:own_rows] * grad_scale
    feature_grad = unpick(rank[:, None], jnp.stack(starts).astype(I32), pieces)
    return feature_grad, weight_grad[:, :dino_cols], weight_grad[:, dino_cols:]


def solution(mesh):
    placed = (
        P(("dp", "rep"), None),
        P(("dp", "rep"), "tsec"),
        P(("dp", "rep"), "tsec"),
        P(None, "tsec"),
        P(None, "tsec"),
        P(("dp", "rep")),
        P(("dp", "rep")),
    )
    return jax.shard_map(
        per_device,
        mesh=mesh,
        in_specs=placed,
        out_specs=(P(("dp", "rep"), None), P("dp", "tsec"), P("dp", "tsec")),
        check_vma=False,
    )
```

time: 453 us -> 322 us (0.71)
  Pallas kernels: 52.5 us -> 257 us
  matrix products: 146 us -> 0 us
  waiting for transfers between devices: 125 us -> 18.8 us
  local copies, waits for them, and re-layouts: 48.9 us -> 5.94 us
  other arithmetic: 27.4 us -> 6.67 us
  starting transfers between devices: 44.2 us -> 28.4 us
    pallas_call x0 -> x7, Pallas kernels: none -> 204 us  [the longest x2 90.7 us: handle_block(): pl.pallas_call(functools.partial(block_kernel, stage), in_specs=[VMEM] *...]
    dot_general x26 -> x0, matrix products: 146 us -> none  [the longest x14 101 us: exact_pick(): return jnp.dot(hit.astype(BF), table, preferred_element_type=F32).astype(BF)]
    ppermute x5 -> x2, waiting for transfers between devices: 55.5 us -> 0.01 us  [per_device(): pieces += [grad, lax.ppermute(grad, 'tsec', swap)]]
    all_to_all x2, waiting for transfers between devices: 69.1 us -> 18.8 us  [exchange(): lax.all_to_all(outbox.reshape(groups, CHUNKS[chunk][1], -1), ('tsec', 'dp...]
    convert_element_type x2 -> x0, local copies, waits for them, and re-layouts: 16.9 us -> none  [exact_pick(): return jnp.dot(hit.astype(BF), table, preferred_element_type=F32).astype(BF)]
    unnamed x56 -> x10, local copies, waits for them, and re-layouts: 13.2 us -> 1.1 us
    another operation x2, local copies, waits for them, and re-layouts: 12.4 us -> 2.07 us  [columns_of(): jnp.stack([order, direct] + [place_in(c, codes) for c in range(len(CHUNKS...]
    all_to_all x2, starting transfers between devices: 36.7 us -> 26.8 us  [exchange(): lax.all_to_all(outbox.reshape(groups, CHUNKS[chunk][1], -1), ('tsec', 'dp...]
  transfers between devices with their start and end apart: 7 -> 4, of which waited for: 5 -> 2; matrix products, arithmetic and copies ran while one was open for 39% -> 3% of each run, Pallas kernels for 12% -> 56%
where the time goes in v2:
time: 322 us; the launch traced here: 318 us
  Pallas kernels  257 us (80%)
  starting transfers between devices  28.4 us (9%)
  waiting for transfers between devices  18.8 us (6%)
  other arithmetic  6.67 us (2%)
  local copies, waits for them, and re-layouts  5.94 us (2%)
    pallas_call x2, Pallas kernels, handle_block(): pl.pallas_call(functools.partial(block_kernel, stage), in_specs=[VMEM] *...  90.7 us
    pallas_call x1, Pallas kernels, forward(): pl.pallas_call(forward_kernel, in_specs=[VMEM] * 8 + [HERE], out_specs=[V...  61.2 us
    pallas_call x1, Pallas kernels, sum_parts(): pl.pallas_call(sum_kernel, out_shape=jax.ShapeDtypeStruct(block, F32), in...  53.2 us
    pallas_call x2, Pallas kernels, local_call(): pl.pallas_call(kernel, grid=(steps,), in_specs=in_specs, out_specs=out_sp...  33 us
    all_to_all x2, starting transfers between devices, exchange(): lax.all_to_all(outbox.reshape(groups, CHUNKS[chunk][1], -1), ('tsec', 'dp...  26.8 us
    pallas_call x2, Pallas kernels, wgrad_part(): pl.pallas_call(functools.partial(wgrad_kernel, len(deltas)), grid=(split,...  18.9 us
    all_to_all x2, waiting for transfers between devices, exchange(): lax.all_to_all(outbox.reshape(groups, CHUNKS[chunk][1], -1), ('tsec', 'dp...  18.8 us
  transfers between devices with their start and end apart: 4, of which 2 were waited for; matrix products, arithmetic and copies ran while one was open for 3% of the time, Pallas kernels for 56%

profile of v2, /device:TPU:1, one launch (start us, length us, event | category | flops | bytes accessed | tf_op | source)
XLA Modules:
  0.0 317.7 jit_solution(2081884245012601764)
XLA Ops:
  0.6 1.3 add_select_fusion.4
  1.9 17.5 %shard_map.94.after_ref = bf16[2048,1344]{1,0:T(8,128)(2,1)} custom-call(s32[1,2048]{1,0:T(1,128)} %bitcast.29, bf16[2048,768]{1,0:T(8,128)(2,1)} %dino_feat_ref.1, bf16[576,2048]{1,0:T(8,128)(2,1)} %bitcast.24, s32[2048]{0:T(1024)} %after_ref.1), custom_call_target="tpu_custom_call" | custom-call | flops 1048576 | bytes 65536 | tf_op jit(solution)/shard_map/pallas_call | solution.py:39
  19.4 13.2 %all-to-all-start = ((bf16[64,32,1344]{2,1,0:T(8,128)(2,1)}), bf16[64,32,1344]{2,1,0:T(8,128)(2,1)}, u32[]{:S(2)}, u32[]{:S(2)}) async-start(bf16[64,32,1344]{2,1,0:T(8,128)(2,1)} %bitcast.22), calls=%async_computation | async-start | bytes 11534336 | tf_op jit(solution)/shard_map/all_to_all | solution.py:490
  32.7 0.0 copy-done.4
  32.7 1.8 convert_reduce_fusion
  34.5 0.0 copy-start.2
  34.5 1.7 select_reduce_fusion
  36.3 0.1 fusion.11
  36.4 0.1 compare_convert_fusion
  36.5 1.0 copy.24.columns_ref
  37.5 61.2 %shard_map.95 = (f32[1024,1280]{1,0:T(8,128)}, bf16[1024,1280]{1,0:T(8,128)(2,1)}, f32[1024,1]{1,0:T(8,128)}, f32[1024,1344]{1,0:T(8,128)}, f32[1024,1344]{1,0:T...) custom-call(s32[1024,4]{1,0:T(8,128)} %copy.24.columns_ref, ...), custom_call_target="tpu_custom_call" | custom-call | flops 30000001024 | bytes 50000000 | tf_op jit(solution)/shard_map/pallas_call | solution.py:154
  98.8 3.2 %all-to-all-done = bf16[64,32,1344]{2,1,0:T(8,128)(2,1)} async-done(((bf16[64,32,1344]{2,1,0:T(8,128)(2,1)}), bf16[64,32,1344]{2,1,0:T(8,128)(2,1)}, u32[]{:S(2)}, u32[]{:S(2)}) %all-to-all-start) | async-done | bytes 5505056 | tf_op jit(solution)/shard_map/all_to_all | solution.py:490
  102.0 13.6 %all-to-all-start.1 = ((bf16[64,32,1344]{2,1,0:T(8,128)(2,1)}), bf16[64,32,1344]{2,1,0:T(8,128)(2,1)}, u32[]{:S(2)}, u32[]{:S(2)}) async-start(bf16[64,32,1344]{2,1,0:T(8,128)(2,1)} %bitcast.23), calls=%async_computation.1 | async-start | bytes 11534336 | tf_op jit(solution)/shard_map/all_to_all | solution.py:490
  115.7 1.0 copy.25.columns_far_ref
  116.8 43.8 %shard_map.96 = (bf16[512,1344]{1,0:T(8,128)(2,1)}, bf16[512,1344]{1,0:T(8,128)(2,1)}, bf16[512,1280]{1,0:T(8,128)(2,1)}, bf16[512,1344]{1,0:T(8,128)(2,1)}, bf16[512,1344]{1,0:T(8,128)(2,1)}) custom-call(s32[1024,4]{1,0:T(8,128)} %copy.24.columns_ref, s32[1024,4]{1,0:T(8,128)} %copy.25.columns_far_ref, f32[1024,1]{1,0:T(8,128)} %get-tuple-element.19.inv_ref, ...), custom_call_target="tpu_custom_call" | custom-call | flops 10000000000 | bytes 30000000 | tf_op jit(solution)/shard_map/pallas_call | solution.py:266
  160.5 9.0 %shard_map.97.refs_2_ = bf16[2,32,48,1344]{3,2,1,0:T(8,128)(2,1)} custom-call(bf16[1024,1280]{1,0:T(8,128)(2,1)} %get-tuple-element.29.bf_ref, bf16[512,1344]{1,0:T(8,128)(2,1)} %get-tuple-element.30.refs_0_, bf16[512,1344]{1,0:T(8,128)(2,1)} %get-tuple-element.31.refs_1_), custom_call_target="tpu_custom_call" | custom-call | flops 1048576 | bytes 65536 | tf_op jit(solution)/shard_map/pallas_call | solution.py:308
  169.5 15.6 %all-to-all-done.1 = bf16[64,32,1344]{2,1,0:T(8,128)(2,1)} async-done(((bf16[64,32,1344]{2,1,0:T(8,128)(2,1)}), bf16[64,32,1344]{2,1,0:T(8,128)(2,1)}, u32[]{:S(2)}, u32[]{:S(2)}) %all-to-all-start.1) | async-done | bytes 5505056 | tf_op jit(solution)/shard_map/all_to_all | solution.py:490
  185.1 46.9 %shard_map.98 = (bf16[512,1344]{1,0:T(8,128)(2,1)}, bf16[512,1344]{1,0:T(8,128)(2,1)}, bf16[512,1280]{1,0:T(8,128)(2,1)}) custom-call(s32[1024,4]{1,0:T(8,128)} %copy.24.columns_ref, s32[1024,4]{1,0:T(8,128)} %copy.25.columns_far_ref, f32[1024,1]{1,0:T(8,128)} %get-tuple-element.19.inv_ref, bf16[2048,1344]{1,0:T(8,128)(2,1)} %bitcast.19.inbox_ref, ...), custom_call_target="tpu_custom_call" | custom-call | flops 10000000000 | bytes 30000000 | tf_op jit(solution)/shard_map/pallas_call | solution.py:266
  232.0 0.1 collective-permute-start.1
  232.1 1.4 collective-permute-start
  233.6 0.0 copy-done.3
  233.6 1.4 copy.28.refs_0_
  234.9 0.7 pad_add_fusion.6.refs_1_
  235.6 9.9 %shard_map.100 = bf16[2,32,48,1344]{3,2,1,0:T(8,128)(2,1)} custom-call(bf16[1024,1280]{1,0:T(8,128)(2,1)} %get-tuple-element.29.bf_ref, bf16[512,1344]{1,0:T(8,128)(2,1)} %get-tuple-element.33.refs_0_, bf16[512,1344]{1,0:T(8,128)(2,1)} %get-tuple-element.34.refs_1_, bf16[2,32,48,1344]{3,2,1,0:T(8,128)(2,1)} %shard_map.97.refs_2_), custom_call_target="tpu_custom_call" | custom-call | flops 1048576 | bytes 65536 | tf_op jit(solution)/shard_map/pallas_call | solution.py:308
  245.5 53.2 %shard_map.101 = f32[48,1344]{1,0:T(8,128)} custom-call(bf16[2,4,4,2,48,1344]{5,4,3,2,1,0:T(8,128)(2,1)} %bitcast.21), custom_call_target="tpu_custom_call" | custom-call | tf_op jit(solution)/shard_map/pallas_call | solution.py:442
  298.7 1.0 slice_multiply_fusion
  299.6 0.7 slice.12
  300.3 0.6 slice.13
  300.9 0.0 collective-permute-done.1.refs_5_
  300.9 0.0 collective-permute-done.refs_3_
  300.9 1.1 copy-done.1
  302.0 15.5 %shard_map.99 = bf16[2048,1280]{1,0:T(8,128)(2,1)} custom-call(s32[2048,1]{1,0:T(8,128)} %copy.28.refs_0_, s32[4]{0:T(128)} %pad_add_fusion.6.refs_1_, bf16[512,1280]{1,0:T(8,128)(2,1)} %get-tuple-element.25.refs_2_, bf16[512,1280]{1,0:T(8,128)(2,1)} %collective-permute-done.refs_3_, bf16[512,1280]{1,0:T(8,128)(2,1)} %get-tuple-element.32.refs_4_, ...), custom_call_target="tpu_custom_call" | custom-call | flops 1048576 | bytes 65536 | tf_op jit(solution)/shard_map/pallas_call | solution.py:39
  (15 shorter events, 0.1 us)
Async XLA Ops:
  19.4 13.3 %copy-start.4 = (s32[2048]{0:T(1024)S(1)}, s32[2048]{0:T(1024)}, u32[]{:S(2)}) copy-start(s32[2048]{0:T(1024)} %param.13) | copy-start | bytes 24580
  19.4 82.5 %all-to-all-start = ((bf16[64,32,1344]{2,1,0:T(8,128)(2,1)}), bf16[64,32,1344]{2,1,0:T(8,128)(2,1)}, u32[]{:S(2)}, u32[]{:S(2)}) async-start(bf16[64,32,1344]{2,1,0:T(8,128)(2,1)} %bitcast.22), calls=%async_computation | async-start | bytes 11534336 | tf_op jit(solution)/shard_map/all_to_all | solution.py:490
  34.5 3.0 copy-start.2
  102.0 83.1 %all-to-all-start.1 = ((bf16[64,32,1344]{2,1,0:T(8,128)(2,1)}), bf16[64,32,1344]{2,1,0:T(8,128)(2,1)}, u32[]{:S(2)}, u32[]{:S(2)}) async-start(bf16[64,32,1344]{2,1,0:T(8,128)(2,1)} %bitcast.23), calls=%async_computation.1 | async-start | bytes 11534336 | tf_op jit(solution)/shard_map/all_to_all | solution.py:490
  185.1 47.0 %copy-start = (bf16[512,1280]{1,0:T(8,128)(2,1)S(1)}, bf16[512,1280]{1,0:T(8,128)(2,1)}, u32[]{:S(2)}) copy-start(bf16[512,1280]{1,0:T(8,128)(2,1)} %get-tuple-element.25.refs_2_) | copy-start | bytes 3932164
  185.1 48.4 %copy-start.3 = (s32[2048]{0:T(1024)S(1)}, s32[2048]{0:T(1024)}, u32[]{:S(2)}) copy-start(s32[2048]{0:T(1024)} %copy-done.2) | copy-start | bytes 24580
  232.0 68.9 %collective-permute-start.1 = (bf16[512,1280]{1,0:T(8,128)(2,1)}, bf16[512,1280]{1,0:T(8,128)(2,1)S(1)}, u32[]{:S(2)}, u32[]{:S(2)}) collective-permute-start(bf16[512,1280]{1,0:T(8,128)(2,1)} %get-tuple-element.32.refs_4_), channel_id=1, source_target_pairs={{0,64},{64,0},{1,65},{65,1},{2,66},{66,2},{3,67},{67,3},{4,68},{68... | collective-permute-start | bytes 3932168 | tf_op jit(solution)/shard_map/ppermute | solution.py:532
  232.1 68.8 %collective-permute-start = (bf16[512,1280]{1,0:T(8,128)(2,1)S(1)}, bf16[512,1280]{1,0:T(8,128)(2,1)}, u32[]{:S(2)}, u32[]{:S(2)}) collective-permute-start(bf16[512,1280]{1,0:T(8,128)(2,1)S(1)} %copy-done), channel_id=1, source_target_pairs={{0,64},{64,0},{1,65},{65,1},{2,66},{66,2},{3,67},{67,3},{4,68},{68... | collective-permute-start | bytes 3932168 | tf_op jit(solution)/shard_map/ppermute | solution.py:532
  300.9 1.1 copy-start.1

commit v3 on v2

--- a/solution.py
+++ b/solution.py
@@ -317,27 +317,6 @@
     )(normed_bf, *deltas, *more)
 
 
-def unpick_kernel(n, rank_ref, starts_ref, *refs):
-    pieces, base, out_ref = refs[:n], refs[n:-1], refs[-1]
-    total = base[0][...].astype(F32) if base else 0.0
-    for i, piece in enumerate(pieces):
-        hit = hits(rank_ref[...], starts_ref[i], piece.shape[0])
-        total = total + jnp.dot(hit, piece[...], preferred_element_type=F32)
-    out_ref[...] = total.astype(BF)
-
-
-def unpick(rank, starts, pieces, base=None):
-    rows, width = rank.shape[0], pieces[0].shape[1]
-    more = [] if base is None else [base]
-    tile = tile_of(rows)
-    return local_call(
-        lambda *refs: unpick_kernel(len(pieces), *refs), rows // tile,
-        [tiles(tile, 1), pl.BlockSpec(memory_space=pltpu.SMEM)] + [whole(p.shape) for p in pieces]
-        + [tiles(tile, width) for _ in more],
-        tiles(tile, width), jax.ShapeDtypeStruct((rows, width), BF),
-        rank, starts, *pieces, *more)
-
-
 def place():
     dp = lax.axis_index("dp")
     x = lax.axis_index("rep") * 2 + lax.axis_index("tsec")
@@ -348,104 +327,150 @@
     return {"tsec": x % 2, "dp": (y * 4 + z) * 2 + c, "rep": x // 2}
 
 
-def sum_kernel(part_ref, out_ref, held, pair, far_y, far_z, far_y2, far_z2, far_x, stage,
-               own_sem, pair_send, pair_recv, send_sem, recv_sem):
+def tail_kernel(scale, part_ref, turned_ref, delta_ref, delta_far_ref, rank_ref, grad0_ref, grad0_far_ref, grad1_ref,
+                feature_ref, dino_ref, siglip_ref,
+                work, pair, far_y, far_z, far_y2, far_z2, far_x, stage, grad1_far,
+                load_sem, pair_send, pair_recv, send_sem, recv_sem):
     x, y, z, c = place()
     t = x % 2
+    sibling, partner = at_place(x, y, z, 1 - c), {"tsec": 1 - t}
+    loads = [[pltpu.make_async_copy(part_ref.at[h, l], work.at[h, l], load_sem.at[4 * h + l]) for l in range(4)]
+             for h in (0, 1)]
+    for h in (0, 1):
+        for load in loads[h]:
+            load.start()
     lines = [[at_place(x, (y + j) % 4, z, c), at_place(x, y, (z + j) % 4, c), at_place((x + j) % 4, y, z, c)]
              for j in (1, 2, 3)]
-    greet([at_place(x, y, z, 1 - c)] + sum(lines, []))
+    greet([sibling] + sum(lines, []))
+    back = remote(grad1_ref, grad1_far, send_sem.at[15], recv_sem.at[15], partner)
+    back.start()
+    rows = feature_ref.shape[1] // 32
+
+    def add_products(h, line):
+        delta = delta_ref if h == 0 else delta_far_ref
+        features = pl.ds(pl.multiple_of(line * 8 * rows, 16), 8 * rows)
+        new = jnp.dot(turned_ref[features], delta[...], preferred_element_type=F32)
+        for b in range(8):
+            old = work[h, line, b // 2, b % 2, :rows].astype(F32)
+            work[h, line, b // 2, b % 2, :rows] = (old + new[b * rows : (b + 1) * rows]).astype(BF)
+
+    def pair_copy(h, j):
+        src = work.at[0, (y + j) % 4, :, 1 - c] if h == 0 else work.at[1, :, (z + j) % 4, 1 - c]
+        return remote(src, pair.at[h, j], pair_send.at[4 * h + j], pair_recv.at[4 * h + j], sibling)
 
     order = (2, 1, 3, 0)
-
-    def pair_copy(k, j, i):
-        line = (y + j) % 4 if k == 0 else (z + j) % 4
-        src = part_ref.at[t, line, :, 1 - c] if k == 0 else part_ref.at[1 - t, :, line, 1 - c]
-        return pltpu.make_async_remote_copy(
-            src_ref=src, dst_ref=pair.at[k, j], send_sem=pair_send.at[i], recv_sem=pair_recv.at[i],
-            device_id=at_place(x, y, z, 1 - c), device_id_type=MESH)
-
-    def own_copy(k, j, i):
-        line = (y + j) % 4 if k == 0 else (z + j) % 4
-        src = part_ref.at[t, line, :, c] if k == 0 else part_ref.at[1 - t, :, line, c]
-        return pltpu.make_async_copy(src, held.at[k, j], own_sem.at[i])
-
-    def line_copy(k, j, i):
-        far = far_y if k == 0 else far_z
-        device = at_place(x, (y + j) % 4, z, c) if k == 0 else at_place(x, y, (z + j) % 4, c)
-        return pltpu.make_async_remote_copy(
-            src_ref=held.at[k, j], dst_ref=far.at[j - 1], send_sem=send_sem.at[i], recv_sem=recv_sem.at[i],
-            device_id=device, device_id_type=MESH)
-
-    steps = [(k, j) for j in order for k in (0, 1)]
-    for i, (k, j) in enumerate(steps):
-        pair_copy(k, j, i).start()
-        own_copy(k, j, i).start()
-    for i, (k, j) in enumerate(steps):
-        own_copy(k, j, i).wait()
-        pair_copy(k, j, i).wait_recv()
+    for load in loads[0]:
+        load.wait()
+    for j in order:
+        add_products(0, (y + j) % 4)
+        pair_copy(0, j).start()
+    for load in loads[1]:
+        load.wait()
+
+    @pl.loop(0, 4)
+    def _(line):
+        add_products(1, line)
+
+    for j in order:
+        pair_copy(1, j).start()
+
+    def line_copy(h, j):
+        far = far_y if h == 0 else far_z
+        device = at_place(x, (y + j) % 4, z, c) if h == 0 else at_place(x, y, (z + j) % 4, c)
+        i = 3 * h + j - 1
+        return remote(pair.at[h, j], far.at[j - 1], send_sem.at[i], recv_sem.at[i], device)
+
+    for j in order:
+        for h in (0, 1):
+            pair_copy(h, j).wait_recv()
+
+            @pl.loop(0, 4)
+            def _(b, h=h, j=j):
+                own = work[0, (y + j) % 4, b, c] if h == 0 else work[1, b, (z + j) % 4, c]
+                pair[h, j, b] = (own.astype(F32) + pair[h, j, b].astype(F32)).astype(BF)
+
+            if j:
+                line_copy(h, j).start()
+
+    count = grad0_ref.shape[0]
+    starts = [(2 * s + side) * count for s in (0, 1) for side in (t, 1 - t)]
+
+    @pl.loop(0, feature_ref.shape[0] // TILE)
+    def _(i):
+        total = 0.0
+        for start, piece in zip(starts, (grad0_ref, grad0_far_ref, grad1_ref)):
+            hit = hits(rank_ref[tile_at(i)], start, count)
+            total = total + jnp.dot(hit, piece[...], preferred_element_type=F32)
+        feature_ref[tile_at(i)] = total.astype(BF)
+
+    for h in (0, 1):
+        for j in order:
+            pair_copy(h, j).wait_send()
+
+    def cross_copy(h, j):
+        far = far_z2 if h == 0 else far_y2
+        b = (z + j) % 4 if h == 0 else (y + j) % 4
+        device = at_place(x, y, b, c) if h == 0 else at_place(x, b, z, c)
+        i = 6 + 3 * h + j - 1
+        return remote(pair.at[h, 0, b], far.at[j - 1], send_sem.at[i], recv_sem.at[i], device)
+
+    for h in (0, 1):
+        far = far_y if h == 0 else far_z
+        for j in (2, 1, 3):
+            line_copy(h, j).wait()
 
         @pl.loop(0, 4)
-        def _(b, k=k, j=j):
-            held[k, j, b] = (held[k, j, b].astype(F32) + pair[k, j, b].astype(F32)).astype(BF)
-
-        if j:
-            line_copy(k, j, k * 3 + j - 1).start()
-    for i, (k, j) in enumerate(steps):
-        pair_copy(k, j, i).wait_send()
-    for k in (0, 1):
+        def _(b, h=h, far=far):
+            pair[h, 0, b] = (pair[h, 0, b].astype(F32) + far[0, b].astype(F32)
+                             + far[1, b].astype(F32) + far[2, b].astype(F32)).astype(BF)
+
         for j in (2, 1, 3):
-            line_copy(k, j, k * 3 + j - 1).wait()
-        far = far_y if k == 0 else far_z
-
-        @pl.loop(0, 4)
-        def _(b, k=k, far=far):
-            held[k, 0, b] = (held[k, 0, b].astype(F32) + far[0, b].astype(F32)
-                             + far[1, b].astype(F32) + far[2, b].astype(F32)).astype(BF)
-
-    def cross_copy(k, j):
-        far = far_z2 if k == 0 else far_y2
-        b = (z + j) % 4 if k == 0 else (y + j) % 4
-        device = at_place(x, y, b, c) if k == 0 else at_place(x, b, z, c)
-        i = 6 + k * 3 + j - 1
-        return pltpu.make_async_remote_copy(
-            src_ref=held.at[k, 0, b], dst_ref=far.at[j - 1], send_sem=send_sem.at[i], recv_sem=recv_sem.at[i],
-            device_id=device, device_id_type=MESH)
-
-    for k in (0, 1):
+            cross_copy(h, j).start()
+
+    back.wait()
+
+    @pl.loop(0, feature_ref.shape[0] // TILE)
+    def _(i):
+        hit = hits(rank_ref[tile_at(i)], starts[3], count)
+        found = jnp.dot(hit, grad1_far[...], preferred_element_type=F32)
+        feature_ref[tile_at(i)] = (feature_ref[tile_at(i)].astype(F32) + found).astype(BF)
+
+    for h in (0, 1):
+        far = far_z2 if h == 0 else far_y2
         for j in (2, 1, 3):
-            cross_copy(k, j).start()
-    for k in (0, 1):
-        for j in (2, 1, 3):
-            cross_copy(k, j).wait()
-        far = far_z2 if k == 0 else far_y2
-        mine = held[k, 0, z] if k == 0 else held[k, 0, y]
-        stage[k] = (mine.astype(F32) + far[0].astype(F32) + far[1].astype(F32) + far[2].astype(F32)).astype(BF)
+            cross_copy(h, j).wait()
+        mine = pair[h, 0, z] if h == 0 else pair[h, 0, y]
+        stage[h] = (mine.astype(F32) + far[0].astype(F32) + far[1].astype(F32) + far[2].astype(F32)).astype(BF)
 
     def x_copy(j):
         device = (x + j) % 4
         i = 12 + j - 1
-        return pltpu.make_async_remote_copy(
-            src_ref=stage.at[device % 2], dst_ref=far_x.at[j - 1], send_sem=send_sem.at[i], recv_sem=recv_sem.at[i],
-            device_id=at_place(device, y, z, c), device_id_type=MESH)
+        return remote(stage.at[(device + x) % 2], far_x.at[j - 1], send_sem.at[i], recv_sem.at[i],
+                      at_place(device, y, z, c))
 
     for j in (2, 1, 3):
         x_copy(j).start()
     for j in (2, 1, 3):
         x_copy(j).wait()
-    out_ref[...] = (stage[t].astype(F32) + far_x[0].astype(F32) + far_x[1].astype(F32) + far_x[2].astype(F32))
-
-
-def sum_parts(part):
-    rows, width = part.shape[-2:]
-    block = (rows, width)
+    total = (stage[0].astype(F32) + far_x[0].astype(F32) + far_x[1].astype(F32) + far_x[2].astype(F32)) * scale
+    dino_ref[...] = total[:rows, : dino_ref.shape[1]]
+    siglip_ref[...] = total[:rows, dino_ref.shape[1] :]
+
+
+def finish(scale, part, turned, delta, delta_far, rank, grads, dino_cols):
+    block = part.shape[-2:]
+    count, features = grads[0].shape
+    own_rows = features // 32
     return pl.pallas_call(
-        sum_kernel,
-        out_shape=jax.ShapeDtypeStruct(block, F32),
-        in_specs=[pl.BlockSpec(memory_space=pl.ANY)],
-        out_specs=pl.BlockSpec(memory_space=pltpu.VMEM),
+        functools.partial(tail_kernel, scale),
+        out_shape=[
+            jax.ShapeDtypeStruct((rank.shape[0], features), BF),
+            jax.ShapeDtypeStruct((own_rows, dino_cols), F32),
+            jax.ShapeDtypeStruct((own_rows, block[1] - dino_cols), F32)],
+        in_specs=[HERE] + [VMEM] * 7,
+        out_specs=[VMEM] * 3,
         scratch_shapes=[
-            pltpu.VMEM((2, 4, 4) + block, BF),
+            pltpu.VMEM((2, 4, 4, 2) + block, BF),
             pltpu.VMEM((2, 4, 4) + block, BF),
             pltpu.VMEM((3, 4) + block, BF),
             pltpu.VMEM((3, 4) + block, BF),
@@ -453,16 +478,18 @@
             pltpu.VMEM((3,) + block, BF),
             pltpu.VMEM((3,) + block, BF),
             pltpu.VMEM((2,) + block, BF),
+            pltpu.VMEM((count, features), BF),
             pltpu.SemaphoreType.DMA((8,)),
             pltpu.SemaphoreType.DMA((8,)),
             pltpu.SemaphoreType.DMA((8,)),
-            pltpu.SemaphoreType.DMA((15,)),
-            pltpu.SemaphoreType.DMA((15,)),
+            pltpu.SemaphoreType.DMA((16,)),
+            pltpu.SemaphoreType.DMA((16,)),
         ],
         compiler_params=pltpu.CompilerParams(
-            collective_id=0, has_side_effects=True, vmem_limit_bytes=58 * 2**20
+            collective_id=0, has_side_effects=True, vmem_limit_bytes=60 * 2**20
         ),
-    )(part)
+        cost_estimate=pl.CostEstimate(flops=10**10, bytes_accessed=5 * 10**7, transcendentals=0),
+    )(part, turned, delta, delta_far, rank, *grads)
 
 
 def per_device(student, dino_feat, siglip_feat, dino_weight, siglip_weight, send_index, recv_index):
@@ -525,20 +552,20 @@
     weights = weights + weights_far
     inboxes = [inbox, exchange(outbox, 1)]
 
-    part, bases, pieces, starts = None, [], [], []
+    turned = normed_bf[quarter:].T
+    bases, grads = [], []
     for stage in (0, 1):
         delta, delta_far, grad, *bases = handle_block(
             stage, columns, columns_far, inv_dev, inboxes[stage], out, out_far, normed, weights, bases)
-        pieces += [grad, lax.ppermute(grad, "tsec", swap)]
-        starts += [(2 * stage + t) * quarter, (2 * stage + 1 - t) * quarter]
-        part = wgrad_part(normed_bf, [delta, delta_far], stage * quarter, n_dp, padded, part)
-        bases = bases + [part]
+        grads.append(grad)
+        if stage == 0:
+            grads.append(lax.ppermute(grad, "tsec", swap))
+            part = wgrad_part(normed_bf, [delta, delta_far], 0, n_dp, padded)
+            bases = bases + [part]
 
     part = part.reshape((2, 4, 4, 2) + part.shape[2:])
     grad_scale = 1.0 / math.sqrt(row_count * groups)
-    weight_grad = sum_parts(part)[:own_rows] * grad_scale
-    feature_grad = unpick(rank[:, None], jnp.stack(starts).astype(I32), pieces)
-    return feature_grad, weight_grad[:, :dino_cols], weight_grad[:, dino_cols:]
+    return tuple(finish(grad_scale, part, turned, delta, delta_far, rank[:, None], grads, dino_cols))
 
 
 def solution(mesh):

time: 322 us -> 305 us (0.947)
  Pallas kernels: 257 us -> 241 us
  local copies, waits for them, and re-layouts: 5.94 us -> 15 us
  waiting for transfers between devices: 18.8 us -> 11.8 us
    pallas_call x2 -> x1, Pallas kernels: 33 us -> 17.5 us  [local_call(): pl.pallas_call(kernel, grid=(steps,), in_specs=in_specs, out_specs=out_sp...]
    pallas_call x2 -> x1, Pallas kernels: 18.9 us -> 8.98 us  [wgrad_part(): pl.pallas_call(functools.partial(wgrad_kernel, len(deltas)), grid=(split,...]
    pallas_call x1, Pallas kernels: 53.2 us -> 62.3 us  [finish(): pl.pallas_call(functools.partial(tail_kernel, scale), out_shape=[jax.Shap...]
    all_to_all x2, waiting for transfers between devices: 18.8 us -> 11.8 us  [exchange(): lax.all_to_all(outbox.reshape(groups, CHUNKS[chunk][1], -1), ('tsec', 'dp...]
    unnamed x10 -> x19, local copies, waits for them, and re-layouts: 1.1 us -> 7.6 us
  transfers between devices with their start and end apart: 4 -> 3, of which waited for: 2 -> 2; matrix products, arithmetic and copies ran while one was open for 3% -> 4% of each run, Pallas kernels for 56% -> 53%
where the time goes in v3:
time: 305 us; the launch traced here: 302 us
  Pallas kernels  241 us (79%)
  starting transfers between devices  28.5 us (9%)
  local copies, waits for them, and re-layouts  15 us (5%)
  waiting for transfers between devices  11.8 us (4%)
  other arithmetic  5.16 us (2%)
    pallas_call x2, Pallas kernels, handle_block(): pl.pallas_call(functools.partial(block_kernel, stage), in_specs=[VMEM] *...  90.7 us
    pallas_call x1, Pallas kernels, finish(): pl.pallas_call(functools.partial(tail_kernel, scale), out_shape=[jax.Shap...  62.3 us
    pallas_call x1, Pallas kernels, forward(): pl.pallas_call(forward_kernel, in_specs=[VMEM] * 8 + [HERE], out_specs=[V...  61.2 us
    all_to_all x2, starting transfers between devices, exchange(): lax.all_to_all(outbox.reshape(groups, CHUNKS[chunk][1], -1), ('tsec', 'dp...  26.8 us
    pallas_call x1, Pallas kernels, local_call(): pl.pallas_call(kernel, grid=(steps,), in_specs=in_specs, out_specs=out_sp...  17.5 us
    all_to_all x2, waiting for transfers between devices, exchange(): lax.all_to_all(outbox.reshape(groups, CHUNKS[chunk][1], -1), ('tsec', 'dp...  11.8 us
    pallas_call x1, Pallas kernels, wgrad_part(): pl.pallas_call(functools.partial(wgrad_kernel, len(deltas)), grid=(split,...  8.98 us
    unnamed x19, local copies, waits for them, and re-layouts  7.6 us
  transfers between devices with their start and end apart: 3, of which 2 were waited for; matrix products, arithmetic and copies ran while one was open for 4% of the time, Pallas kernels for 53%

profile of v3, /device:TPU:1, one launch (start us, length us, event | category | flops | bytes accessed | tf_op | source)
XLA Modules:
  0.0 302.1 jit_solution(3695741381418290899)
XLA Ops:
  0.6 1.3 add_select_fusion.4
  1.9 17.5 %shard_map.94.after_ref = bf16[2048,1344]{1,0:T(8,128)(2,1)} custom-call(s32[1,2048]{1,0:T(1,128)} %bitcast.27, bf16[2048,768]{1,0:T(8,128)(2,1)} %dino_feat_ref.1, bf16[576,2048]{1,0:T(8,128)(2,1)} %bitcast.22, s32[2048]{0:T(1024)} %after_ref.1), custom_call_target="tpu_custom_call" | custom-call | flops 1048576 | bytes 65536 | tf_op jit(solution)/shard_map/pallas_call | solution.py:39
  19.4 13.2 %all-to-all-start = ((bf16[64,32,1344]{2,1,0:T(8,128)(2,1)}), bf16[64,32,1344]{2,1,0:T(8,128)(2,1)}, u32[]{:S(2)}, u32[]{:S(2)}) async-start(bf16[64,32,1344]{2,1,0:T(8,128)(2,1)} %bitcast.20), calls=%async_computation | async-start | bytes 11534336 | tf_op jit(solution)/shard_map/all_to_all | solution.py:517
  32.7 0.0 copy-done.6
  32.7 1.8 convert_reduce_fusion
  34.5 0.0 copy-start.4
  34.5 1.7 select_reduce_fusion
  36.3 0.1 fusion.11
  36.5 1.0 copy.26.columns_ref
  37.5 0.0 copy-done.4
  37.5 61.2 %shard_map.95 = (f32[1024,1280]{1,0:T(8,128)}, bf16[1024,1280]{1,0:T(8,128)(2,1)}, f32[1024,1]{1,0:T(8,128)}, f32[1024,1344]{1,0:T(8,128)}, f32[1024,1344]{1,0:T...) custom-call(s32[1024,4]{1,0:T(8,128)} %copy.26.columns_ref, ...), custom_call_target="tpu_custom_call" | custom-call | flops 30000001024 | bytes 50000000 | tf_op jit(solution)/shard_map/pallas_call | solution.py:154
  98.7 3.3 %all-to-all-done = bf16[64,32,1344]{2,1,0:T(8,128)(2,1)} async-done(((bf16[64,32,1344]{2,1,0:T(8,128)(2,1)}), bf16[64,32,1344]{2,1,0:T(8,128)(2,1)}, u32[]{:S(2)}, u32[]{:S(2)}) %all-to-all-start) | async-done | bytes 5505056 | tf_op jit(solution)/shard_map/all_to_all | solution.py:517
  102.0 13.6 %all-to-all-start.1 = ((bf16[64,32,1344]{2,1,0:T(8,128)(2,1)}), bf16[64,32,1344]{2,1,0:T(8,128)(2,1)}, u32[]{:S(2)}, u32[]{:S(2)}) async-start(bf16[64,32,1344]{2,1,0:T(8,128)(2,1)} %bitcast.21), calls=%async_computation.1 | async-start | bytes 11534336 | tf_op jit(solution)/shard_map/all_to_all | solution.py:517
  115.6 0.0 copy-start.5
  115.7 1.0 copy.28.columns_far_ref
  116.8 2.8 copy.29
  119.6 1.3 copy.32.rank_ref
  120.9 43.9 %shard_map.96 = (bf16[512,1344]{1,0:T(8,128)(2,1)}, bf16[512,1344]{1,0:T(8,128)(2,1)}, bf16[512,1280]{1,0:T(8,128)(2,1)}, bf16[512,1344]{1,0:T(8,128)(2,1)}, bf16[512,1344]{1,0:T(8,128)(2,1)}) custom-call(s32[1024,4]{1,0:T(8,128)} %copy.26.columns_ref, s32[1024,4]{1,0:T(8,128)} %copy.28.columns_far_ref, f32[1024,1]{1,0:T(8,128)} %get-tuple-element.20.inv_ref, ...), custom_call_target="tpu_custom_call" | custom-call | flops 10000000000 | bytes 30000000 | tf_op jit(solution)/shard_map/pallas_call | solution.py:266
  164.9 1.7 collective-permute-start
  166.6 1.2 slice_bitcast_fusion.turned_ref
  167.8 9.0 %shard_map.97.refs_2_ = bf16[2,32,48,1344]{3,2,1,0:T(8,128)(2,1)} custom-call(bf16[1024,1280]{1,0:T(8,128)(2,1)} %get-tuple-element.19.bf_ref, bf16[512,1344]{1,0:T(8,128)(2,1)} %get-tuple-element.26.refs_0_, bf16[512,1344]{1,0:T(8,128)(2,1)} %get-tuple-element.27.refs_1_), custom_call_target="tpu_custom_call" | custom-call | flops 1048576 | bytes 65536 | tf_op jit(solution)/shard_map/pallas_call | solution.py:308
  176.8 8.5 %all-to-all-done.1 = bf16[64,32,1344]{2,1,0:T(8,128)(2,1)} async-done(((bf16[64,32,1344]{2,1,0:T(8,128)(2,1)}), bf16[64,32,1344]{2,1,0:T(8,128)(2,1)}, u32[]{:S(2)}, u32[]{:S(2)}) %all-to-all-start.1) | async-done | bytes 5505056 | tf_op jit(solution)/shard_map/all_to_all | solution.py:517
  185.3 46.7 %shard_map.98 = (bf16[512,1344]{1,0:T(8,128)(2,1)}, bf16[512,1344]{1,0:T(8,128)(2,1)}, bf16[512,1280]{1,0:T(8,128)(2,1)}) custom-call(s32[1024,4]{1,0:T(8,128)} %copy.26.columns_ref, s32[1024,4]{1,0:T(8,128)} %copy.28.columns_far_ref, f32[1024,1]{1,0:T(8,128)} %get-tuple-element.20.inv_ref, bf16[2048,1344]{1,0:T(8,128)(2,1)} %bitcast.16.inbox_ref, ...), custom_call_target="tpu_custom_call" | custom-call | flops 10000000000 | bytes 30000000 | tf_op jit(solution)/shard_map/pallas_call | solution.py:266
  232.0 0.0 collective-permute-done.grad0_far_ref
  232.0 0.0 copy-start.7
  232.0 1.1 copy-done.7
  233.1 62.3 %shard_map.99 = (bf16[2048,1280]{1,0:T(8,128)(2,1)}, f32[40,768]{1,0:T(8,128)}, f32[40,576]{1,0:T(8,128)}) custom-call(bf16[2,4,4,2,48,1344]{5,4,3,2,1,0:T(8,128)(2,1)} %bitcast.19, bf16[1280,512]{1,0:T(8,128)(2,1)} %slice_bitcast_fusion.turned_ref, bf16[512,1344]{1,0:T(8,128)(2,1)} %get-tuple-element.31.delta_ref, ...), custom_call_target="tpu_custom_call" | custom-call | flops 10000000000 | bytes 50000000 | tf_op jit(solution)/shard_map/pallas_call | solution.py:464
  295.4 5.2 %copy.36 = bf16[2048,1280]{1,0:T(8,128)(2,1)} copy(bf16[2048,1280]{1,0:T(8,128)(2,1)} %get-tuple-element.57) | data formatting | bytes 10485760
  300.6 0.0 copy-done.2
  300.6 0.6 copy.37
  301.3 0.0 copy-done.3
  301.3 0.6 copy.38
  (19 shorter events, 0.2 us)
Async XLA Ops:
  19.4 13.2 %copy-start.6 = (s32[2048]{0:T(1024)S(1)}, s32[2048]{0:T(1024)}, u32[]{:S(2)}) copy-start(s32[2048]{0:T(1024)} %param.13) | copy-start | bytes 24580
  19.4 82.5 %all-to-all-start = ((bf16[64,32,1344]{2,1,0:T(8,128)(2,1)}), bf16[64,32,1344]{2,1,0:T(8,128)(2,1)}, u32[]{:S(2)}, u32[]{:S(2)}) async-start(bf16[64,32,1344]{2,1,0:T(8,128)(2,1)} %bitcast.20), calls=%async_computation | async-start | bytes 11534336 | tf_op jit(solution)/shard_map/all_to_all | solution.py:517
  34.5 3.0 copy-start.4
  102.0 14.8 %copy-start = (bf16[1024,1280]{1,0:T(8,128)(2,1)S(1)}, bf16[1024,1280]{1,0:T(8,128)(2,1)}, u32[]{:S(2)}) copy-start(bf16[1024,1280]{1,0:T(8,128)(2,1)} %get-tuple-element.19.bf_ref) | copy-start | bytes 7864324
  102.0 83.3 %all-to-all-start.1 = ((bf16[64,32,1344]{2,1,0:T(8,128)(2,1)}), bf16[64,32,1344]{2,1,0:T(8,128)(2,1)}, u32[]{:S(2)}, u32[]{:S(2)}) async-start(bf16[64,32,1344]{2,1,0:T(8,128)(2,1)} %bitcast.21), calls=%async_computation.1 | async-start | bytes 11534336 | tf_op jit(solution)/shard_map/all_to_all | solution.py:517
  115.6 4.0 %copy-start.5 = (s32[2048]{0:T(1024)S(1)}, s32[2048]{0:T(1024)}, u32[]{:S(2)}) copy-start(s32[2048]{0:T(1024)} %copy-done.4) | copy-start | bytes 24580
  120.9 45.7 %copy-start.1 = (bf16[1024,1280]{0,1:T(8,128)(2,1)S(1)}, bf16[1024,1280]{0,1:T(8,128)(2,1)}, u32[]{:S(2)}) copy-start(bf16[1024,1280]{0,1:T(8,128)(2,1)} %copy.29) | copy-start | bytes 7864324
  164.9 67.1 %collective-permute-start = (bf16[512,1280]{1,0:T(8,128)(2,1)}, bf16[512,1280]{1,0:T(8,128)(2,1)S(1)}, u32[]{:S(2)}, u32[]{:S(2)}) collective-permute-start(bf16[512,1280]{1,0:T(8,128)(2,1)} %get-tuple-element.33.grad0_ref), channel_id=1, source_target_pairs={{0,64},{64,0},{1,65},{65,1},{2,66},{66,2},{3,67},{67,3},{4,68},{68... | collective-permute-start | bytes 3932168 | tf_op jit(solution)/shard_map/ppermute | solution.py:562
  232.0 1.1 copy-start.7
  295.4 5.2 %copy-start.2 = (f32[40,768]{1,0:T(8,128)S(1)}, f32[40,768]{1,0:T(8,128)}, u32[]{:S(2)}) copy-start(f32[40,768]{1,0:T(8,128)} %get-tuple-element.58) | copy-start | bytes 368644
  295.4 5.9 %copy-start.3 = (f32[40,576]{1,0:T(8,128)S(1)}, f32[40,576]{1,0:T(8,128)}, u32[]{:S(2)}) copy-start(f32[40,576]{1,0:T(8,128)} %get-tuple-element.59) | copy-start | bytes 276484

commit v4 on v3

--- a/solution.py
+++ b/solution.py
@@ -83,8 +83,8 @@
     pl.semaphore_wait(barrier, len(devices))
 
 
-def tile_at(i, start=0):
-    return pl.ds(pl.multiple_of(start + i * TILE, TILE), TILE)
+def tile_at(i, start=0, tile=TILE):
+    return pl.ds(pl.multiple_of(start + i * tile, tile), tile)
 
 
 def remote(src, dst, send_sem, recv_sem, device):
@@ -188,17 +188,21 @@
         delta_ref, delta_far_ref, grad_ref, base_far_ref, base_ref = refs[:5]
         refs = refs[5:]
     else:
-        base_far_ref, base_ref, _, delta_ref, delta_far_ref, grad_ref = refs[:6]
-        refs = refs[6:]
+        base_far_in, base_in, _, delta_ref, delta_far_ref, grad_ref = refs[:6]
+        base_far_ref, base_ref = refs[-2:]
+        refs = refs[6:-2]
     table, out, out_far, normed_all, dino_w, siglip_w, dino_far_w, siglip_far_w, sent, came, near_all = refs[:11]
     copy_sem, send_sem, recv_sem = refs[11:]
     rows = delta_ref.shape[0]
     first = stage * rows
     cols = dino_w.shape[1]
+    tile = TILE // (1 + stage)
+    at = functools.partial(tile_at, tile=tile)
+    bases = ((base_far_in, base_far_ref), (base_in, base_ref)) if stage else ()
     loads = [
         pltpu.make_async_copy(src, dst, copy_sem.at[i])
-        for i, (src, dst) in enumerate((
-            (inbox_ref, table), (dino_ref, dino_w), (siglip_ref, siglip_w), (dino_far_ref, dino_far_w),
+        for i, (src, dst) in enumerate(((inbox_ref, table),) + bases + (
+            (dino_ref, dino_w), (siglip_ref, siglip_w), (dino_far_ref, dino_far_w),
             (siglip_far_ref, siglip_far_w), (out_ref.at[pl.ds(first, rows)], out),
             (out_far_ref.at[pl.ds(first, rows)], out_far), (normed_ref.at[pl.ds(first, rows)], normed_all)))
     ]
@@ -208,52 +212,53 @@
     greet([partner])
 
     def swap(i):
-        return remote(sent.at[tile_at(i)], came.at[tile_at(i)], send_sem.at[i], recv_sem.at[i], partner)
+        return remote(sent.at[at(i)], came.at[at(i)], send_sem.at[i], recv_sem.at[i], partner)
 
     def look_up(column):
-        hit = (column == lax.broadcasted_iota(I32, (TILE, table.shape[0]), 1)).astype(BF)
+        hit = (column == lax.broadcasted_iota(I32, (tile, table.shape[0]), 1)).astype(BF)
         return jnp.dot(hit, table[...], preferred_element_type=F32)
 
-    loads[0].wait()
-    steps = rows // TILE
+    for load in loads[: 1 + len(bases)]:
+        load.wait()
+    steps = rows // tile
     for i in range(steps):
-        found = look_up(columns_far_ref[tile_at(i, first), 2 + stage : 3 + stage])
+        found = look_up(columns_far_ref[at(i, first), 2 + stage : 3 + stage])
         if stage:
-            found = found + base_far_ref[tile_at(i)].astype(F32)
-        sent[tile_at(i)] = found.astype(BF)
+            found = found + base_far_ref[at(i)].astype(F32)
+        sent[at(i)] = found.astype(BF)
         swap(i).start()
     for i in range(steps):
-        found = look_up(columns_ref[tile_at(i, first), 2 + stage : 3 + stage])
+        found = look_up(columns_ref[at(i, first), 2 + stage : 3 + stage])
         if stage:
-            found = found + base_ref[tile_at(i)].astype(F32)
-        near_all[tile_at(i)] = found.astype(BF)
+            found = found + base_ref[at(i)].astype(F32)
+        near_all[at(i)] = found.astype(BF)
     if stage == 0:
         for i in range(steps):
-            base_far_ref[tile_at(i)] = look_up(columns_far_ref[tile_at(i, rows), 2:3]).astype(BF)
-            base_ref[tile_at(i)] = look_up(columns_ref[tile_at(i, rows), 2:3]).astype(BF)
-    for load in loads[1:]:
+            base_far_ref[at(i)] = look_up(columns_far_ref[at(i, rows), 2:3]).astype(BF)
+            base_ref[at(i)] = look_up(columns_ref[at(i, rows), 2:3]).astype(BF)
+    for load in loads[1 + len(bases) :]:
         load.wait()
     for i in range(steps):
         swap(i).wait_recv()
-        near, far = near_all[tile_at(i)].astype(F32), came[tile_at(i)].astype(F32)
-        direct = columns_ref[tile_at(i, first), 1:2] > 0
+        near, far = near_all[at(i)].astype(F32), came[at(i)].astype(F32)
+        direct = columns_ref[at(i, first), 1:2] > 0
         own = jnp.where(direct, near, far)
         other = jnp.where(direct, far, near)
-        y, y_far = out[tile_at(i)], out_far[tile_at(i)]
+        y, y_far = out[at(i)], out_far[at(i)]
         dino = head_delta([y[:, :cols], y_far[:, :cols]], [own[:, :cols], other[:, :cols]], float(E1))
         siglip = head_delta([y[:, cols:], y_far[:, cols:]], [own[:, cols:], other[:, cols:]], float(E2))
         for delta, d, g in ((delta_ref, dino[0], siglip[0]), (delta_far_ref, dino[1], siglip[1])):
-            delta[tile_at(i), :cols] = d
-            delta[tile_at(i), cols:] = g
+            delta[at(i), :cols] = d
+            delta[at(i), cols:] = g
         part = back_product(dino[0], dino_w[...]) + jnp.dot(siglip[0], siglip_w[...], preferred_element_type=F32)
         part_far = back_product(dino[1], dino_far_w[...]) + jnp.dot(
             siglip[1], siglip_far_w[...], preferred_element_type=F32)
         normed_grad = part.astype(BF).astype(F32) + part_far.astype(BF).astype(F32)
-        normed = normed_all[tile_at(i)]
+        normed = normed_all[at(i)]
         grad_mean = jnp.mean(normed_grad, 1, keepdims=True)
         grad_proj = jnp.mean(normed_grad * normed, 1, keepdims=True)
-        inv_dev = inv_ref[tile_at(i, first)]
-        grad_ref[tile_at(i)] = ((normed_grad - grad_mean - normed * grad_proj) * inv_dev).astype(BF)
+        inv_dev = inv_ref[at(i, first)]
+        grad_ref[at(i)] = ((normed_grad - grad_mean - normed * grad_proj) * inv_dev).astype(BF)
     for i in range(steps):
         swap(i).wait_send()
 
@@ -263,17 +268,18 @@
     width = inbox.shape[1]
     wide, thin = jax.ShapeDtypeStruct((rows, width), BF), jax.ShapeDtypeStruct((rows, features), BF)
     shapes = [wide, wide, thin] + ([wide, wide] if stage == 0 else [])
+    steps = rows // TILE * (1 + stage)
     return pl.pallas_call(
         functools.partial(block_kernel, stage),
-        in_specs=[VMEM] * 3 + [HERE] * 8 + ([VMEM, VMEM, HERE] if stage else []),
+        in_specs=[VMEM] * 3 + [HERE] * (11 if stage else 8),
         out_specs=[VMEM] * len(shapes),
         out_shape=shapes,
         scratch_shapes=[
             pltpu.VMEM(inbox.shape, BF), pltpu.VMEM((rows, width), F32), pltpu.VMEM((rows, width), F32),
             pltpu.VMEM((rows, features), F32)] + [pltpu.VMEM(w.shape, BF) for w in weights] + [
             pltpu.VMEM((rows, width), BF), pltpu.VMEM((rows, width), BF), pltpu.VMEM((rows, width), BF),
-            pltpu.SemaphoreType.DMA((8,)), pltpu.SemaphoreType.DMA((rows // TILE,)),
-            pltpu.SemaphoreType.DMA((rows // TILE,))],
+            pltpu.SemaphoreType.DMA((10,)), pltpu.SemaphoreType.DMA((steps,)), pltpu.SemaphoreType.DMA((steps,))]
+        + [pltpu.VMEM((rows, width), BF) for _ in range(2 * stage)],
         compiler_params=pltpu.CompilerParams(
             collective_id=2 + stage, has_side_effects=True, vmem_limit_bytes=60 * 2**20),
         cost_estimate=pl.CostEstimate(flops=10**10, bytes_accessed=3 * 10**7, transcendentals=0),
@@ -334,11 +340,18 @@
     x, y, z, c = place()
     t = x % 2
     sibling, partner = at_place(x, y, z, 1 - c), {"tsec": 1 - t}
-    loads = [[pltpu.make_async_copy(part_ref.at[h, l], work.at[h, l], load_sem.at[4 * h + l]) for l in range(4)]
-             for h in (0, 1)]
-    for h in (0, 1):
-        for load in loads[h]:
-            load.start()
+    steps = [(h, j) for j in (2, 1, 3, 0) for h in (0, 1)]
+
+    def line_of(h, j):
+        return (y + j) % 4 if h == 0 else (z + j) % 4
+
+    def load(h, j):
+        line = line_of(h, j)
+        src, dst = (r.at[0, line] if h == 0 else r.at[1, :, line] for r in (part_ref, work))
+        return pltpu.make_async_copy(src, dst, load_sem.at[4 * h + j])
+
+    for h, j in steps:
+        load(h, j).start()
     lines = [[at_place(x, (y + j) % 4, z, c), at_place(x, y, (z + j) % 4, c), at_place((x + j) % 4, y, z, c)]
              for j in (1, 2, 3)]
     greet([sibling] + sum(lines, []))
@@ -346,33 +359,20 @@
     back.start()
     rows = feature_ref.shape[1] // 32
 
-    def add_products(h, line):
+    def add_products(h, j):
         delta = delta_ref if h == 0 else delta_far_ref
+        line = line_of(h, j)
         features = pl.ds(pl.multiple_of(line * 8 * rows, 16), 8 * rows)
-        new = jnp.dot(turned_ref[features], delta[...], preferred_element_type=F32)
+        new = jnp.dot(turned_ref[h, features], delta[...], preferred_element_type=F32)
         for b in range(8):
-            old = work[h, line, b // 2, b % 2, :rows].astype(F32)
-            work[h, line, b // 2, b % 2, :rows] = (old + new[b * rows : (b + 1) * rows]).astype(BF)
+            at = (0, line, b // 2, b % 2) if h == 0 else (1, b // 2, line, b % 2)
+            old = work[at + (slice(0, rows),)].astype(F32)
+            work[at + (slice(0, rows),)] = (old + new[b * rows : (b + 1) * rows]).astype(BF)
 
     def pair_copy(h, j):
-        src = work.at[0, (y + j) % 4, :, 1 - c] if h == 0 else work.at[1, :, (z + j) % 4, 1 - c]
+        line = line_of(h, j)
+        src = work.at[0, line, :, 1 - c] if h == 0 else work.at[1, :, line, 1 - c]
         return remote(src, pair.at[h, j], pair_send.at[4 * h + j], pair_recv.at[4 * h + j], sibling)
-
-    order = (2, 1, 3, 0)
-    for load in loads[0]:
-        load.wait()
-    for j in order:
-        add_products(0, (y + j) % 4)
-        pair_copy(0, j).start()
-    for load in loads[1]:
-        load.wait()
-
-    @pl.loop(0, 4)
-    def _(line):
-        add_products(1, line)
-
-    for j in order:
-        pair_copy(1, j).start()
 
     def line_copy(h, j):
         far = far_y if h == 0 else far_z
@@ -380,17 +380,27 @@
         i = 3 * h + j - 1
         return remote(pair.at[h, j], far.at[j - 1], send_sem.at[i], recv_sem.at[i], device)
 
-    for j in order:
-        for h in (0, 1):
-            pair_copy(h, j).wait_recv()
-
-            @pl.loop(0, 4)
-            def _(b, h=h, j=j):
-                own = work[0, (y + j) % 4, b, c] if h == 0 else work[1, b, (z + j) % 4, c]
-                pair[h, j, b] = (own.astype(F32) + pair[h, j, b].astype(F32)).astype(BF)
-
-            if j:
-                line_copy(h, j).start()
+    def combine(h, j):
+        pair_copy(h, j).wait_recv()
+        line = line_of(h, j)
+
+        @pl.loop(0, 4)
+        def _(b):
+            own = work[0, line, b, c] if h == 0 else work[1, b, line, c]
+            pair[h, j, b] = (own.astype(F32) + pair[h, j, b].astype(F32)).astype(BF)
+
+        if j:
+            line_copy(h, j).start()
+
+    lag = 2
+    for i, (h, j) in enumerate(steps):
+        load(h, j).wait()
+        add_products(h, j)
+        pair_copy(h, j).start()
+        if i >= lag:
+            combine(*steps[i - lag])
+    for h, j in steps[-lag:]:
+        combine(h, j)
 
     count = grad0_ref.shape[0]
     starts = [(2 * s + side) * count for s in (0, 1) for side in (t, 1 - t)]
@@ -403,9 +413,8 @@
             total = total + jnp.dot(hit, piece[...], preferred_element_type=F32)
         feature_ref[tile_at(i)] = total.astype(BF)
 
-    for h in (0, 1):
-        for j in order:
-            pair_copy(h, j).wait_send()
+    for h, j in steps:
+        pair_copy(h, j).wait_send()
 
     def cross_copy(h, j):
         far = far_z2 if h == 0 else far_y2
@@ -553,6 +562,8 @@
     inboxes = [inbox, exchange(outbox, 1)]
 
     turned = normed_bf[quarter:].T
+    by_z = turned.reshape(4, 4, -1, quarter).transpose(1, 0, 2, 3).reshape(turned.shape)
+    turned = jnp.stack([turned, by_z])
     bases, grads = [], []
     for stage in (0, 1):
         delta, delta_far, grad, *bases = handle_block(

time: 305 us -> 300 us (0.984)
  Pallas kernels: 241 us -> 237 us
    unnamed x19 -> x17, local copies, waits for them, and re-layouts: 7.6 us -> 6.55 us
  transfers between devices with their start and end apart: 3 -> 3, of which waited for: 2 -> 2; matrix products, arithmetic and copies ran while one was open for 4% -> 4% of each run, Pallas kernels for 53% -> 54%
where the time goes in v4:
time: 300 us; the launch traced here: 297 us
  Pallas kernels  237 us (79%)
  starting transfers between devices  28.2 us (9%)
  local copies, waits for them, and re-layouts  13.1 us (4%)
  waiting for transfers between devices  11 us (4%)
  other arithmetic  6.88 us (2%)
    pallas_call x2, Pallas kernels, handle_block(): pl.pallas_call(functools.partial(block_kernel, stage), in_specs=[VMEM] *...  88.9 us
    pallas_call x1, Pallas kernels, forward(): pl.pallas_call(forward_kernel, in_specs=[VMEM] * 8 + [HERE], out_specs=[V...  61.2 us
    pallas_call x1, Pallas kernels, finish(): pl.pallas_call(functools.partial(tail_kernel, scale), out_shape=[jax.Shap...  60.2 us
    all_to_all x2, starting transfers between devices, exchange(): lax.all_to_all(outbox.reshape(groups, CHUNKS[chunk][1], -1), ('tsec', 'dp...  26.4 us
    pallas_call x1, Pallas kernels, local_call(): pl.pallas_call(kernel, grid=(steps,), in_specs=in_specs, out_specs=out_sp...  17.5 us
    all_to_all x2, waiting for transfers between devices, exchange(): lax.all_to_all(outbox.reshape(groups, CHUNKS[chunk][1], -1), ('tsec', 'dp...  11 us
    pallas_call x1, Pallas kernels, wgrad_part(): pl.pallas_call(functools.partial(wgrad_kernel, len(deltas)), grid=(split,...  8.75 us
    unnamed x17, local copies, waits for them, and re-layouts  6.55 us
  transfers between devices with their start and end apart: 3, of which 2 were waited for; matrix products, arithmetic and copies ran while one was open for 4% of the time, Pallas kernels for 54%

profile of v4, /device:TPU:1, one launch (start us, length us, event | category | flops | bytes accessed | tf_op | source)
XLA Modules:
  0.0 296.8 jit_solution(10088622951893436871)
XLA Ops:
  0.6 1.3 add_select_fusion.4
  1.9 17.5 %shard_map.94.after_ref = bf16[2048,1344]{1,0:T(8,128)(2,1)} custom-call(s32[1,2048]{1,0:T(1,128)} %bitcast.36, bf16[2048,768]{1,0:T(8,128)(2,1)} %dino_feat_ref.1, bf16[576,2048]{1,0:T(8,128)(2,1)} %bitcast.31, s32[2048]{0:T(1024)} %after_ref.1), custom_call_target="tpu_custom_call" | custom-call | flops 1048576 | bytes 65536 | tf_op jit(solution)/shard_map/pallas_call | solution.py:39
  19.5 12.8 %all-to-all-start = ((bf16[64,32,1344]{2,1,0:T(8,128)(2,1)}), bf16[64,32,1344]{2,1,0:T(8,128)(2,1)}, u32[]{:S(2)}, u32[]{:S(2)}) async-start(bf16[64,32,1344]{2,1,0:T(8,128)(2,1)} %bitcast.27), calls=%async_computation | async-start | bytes 11534336 | tf_op jit(solution)/shard_map/all_to_all | solution.py:526
  32.3 0.0 copy-done.6
  32.4 1.8 convert_reduce_fusion
  34.2 0.0 copy-start.4
  34.2 1.7 select_reduce_fusion
  35.9 0.1 fusion.11
  36.1 1.0 copy.29.columns_ref
  37.2 0.0 copy-done.4
  37.2 61.2 %shard_map.95 = (f32[1024,1280]{1,0:T(8,128)}, bf16[1024,1280]{1,0:T(8,128)(2,1)}, f32[1024,1]{1,0:T(8,128)}, f32[1024,1344]{1,0:T(8,128)}, f32[1024,1344]{1,0:T...) custom-call(s32[1024,4]{1,0:T(8,128)} %copy.29.columns_ref, ...), custom_call_target="tpu_custom_call" | custom-call | flops 30000001024 | bytes 50000000 | tf_op jit(solution)/shard_map/pallas_call | solution.py:154
  98.4 3.2 %all-to-all-done = bf16[64,32,1344]{2,1,0:T(8,128)(2,1)} async-done(((bf16[64,32,1344]{2,1,0:T(8,128)(2,1)}), bf16[64,32,1344]{2,1,0:T(8,128)(2,1)}, u32[]{:S(2)}, u32[]{:S(2)}) %all-to-all-start) | async-done | bytes 5505056 | tf_op jit(solution)/shard_map/all_to_all | solution.py:526
  101.6 13.6 %all-to-all-start.1 = ((bf16[64,32,1344]{2,1,0:T(8,128)(2,1)}), bf16[64,32,1344]{2,1,0:T(8,128)(2,1)}, u32[]{:S(2)}, u32[]{:S(2)}) async-start(bf16[64,32,1344]{2,1,0:T(8,128)(2,1)} %bitcast.28), calls=%async_computation.1 | async-start | bytes 11534336 | tf_op jit(solution)/shard_map/all_to_all | solution.py:526
  115.4 1.0 copy.31.columns_far_ref
  116.4 0.0 copy-done
  116.4 2.8 copy.32
  119.2 0.0 copy-start.1
  119.2 44.0 %shard_map.96 = (bf16[512,1344]{1,0:T(8,128)(2,1)}, bf16[512,1344]{1,0:T(8,128)(2,1)}, bf16[512,1280]{1,0:T(8,128)(2,1)}, bf16[512,1344]{1,0:T(8,128)(2,1)}, bf16[512,1344]{1,0:T(8,128)(2,1)}) custom-call(s32[1024,4]{1,0:T(8,128)} %copy.29.columns_ref, s32[1024,4]{1,0:T(8,128)} %copy.31.columns_far_ref, f32[1024,1]{1,0:T(8,128)} %get-tuple-element.20.inv_ref, ...), custom_call_target="tpu_custom_call" | custom-call | flops 10000000000 | bytes 30000000 | tf_op jit(solution)/shard_map/pallas_call | solution.py:272
  163.3 0.0 copy-start.5
  163.3 1.7 collective-permute-start
  165.0 0.2 slice_bitcast_fusion
  165.2 0.1 copy.33
  165.4 1.4 copy.36.rank_ref
  166.7 1.7 pad_maximum_fusion.turned_ref
  168.4 8.7 %shard_map.97.refs_2_ = bf16[2,32,48,1344]{3,2,1,0:T(8,128)(2,1)} custom-call(bf16[1024,1280]{1,0:T(8,128)(2,1)} %get-tuple-element.19.bf_ref, bf16[512,1344]{1,0:T(8,128)(2,1)} %get-tuple-element.26.refs_0_, bf16[512,1344]{1,0:T(8,128)(2,1)} %get-tuple-element.27.refs_1_), custom_call_target="tpu_custom_call" | custom-call | flops 1048576 | bytes 65536 | tf_op jit(solution)/shard_map/pallas_call | solution.py:314
  177.2 7.7 %all-to-all-done.1 = bf16[64,32,1344]{2,1,0:T(8,128)(2,1)} async-done(((bf16[64,32,1344]{2,1,0:T(8,128)(2,1)}), bf16[64,32,1344]{2,1,0:T(8,128)(2,1)}, u32[]{:S(2)}, u32[]{:S(2)}) %all-to-all-start.1) | async-done | bytes 5505056 | tf_op jit(solution)/shard_map/all_to_all | solution.py:526
  184.9 44.9 %shard_map.98 = (bf16[512,1344]{1,0:T(8,128)(2,1)}, bf16[512,1344]{1,0:T(8,128)(2,1)}, bf16[512,1280]{1,0:T(8,128)(2,1)}) custom-call(s32[1024,4]{1,0:T(8,128)} %copy.29.columns_ref, s32[1024,4]{1,0:T(8,128)} %copy.31.columns_far_ref, f32[1024,1]{1,0:T(8,128)} %get-tuple-element.20.inv_ref, bf16[2048,1344]{1,0:T(8,128)(2,1)} %bitcast.20.inbox_ref, ...), custom_call_target="tpu_custom_call" | custom-call | flops 10000000000 | bytes 30000000 | tf_op jit(solution)/shard_map/pallas_call | solution.py:272
  229.8 0.0 collective-permute-done.grad0_far_ref
  229.8 60.2 %shard_map.99 = (bf16[2048,1280]{1,0:T(8,128)(2,1)}, f32[40,768]{1,0:T(8,128)}, f32[40,576]{1,0:T(8,128)}) custom-call(bf16[2,4,4,2,48,1344]{5,4,3,2,1,0:T(8,128)(2,1)} %bitcast.26, bf16[2,1280,512]{2,1,0:T(8,128)(2,1)} %pad_maximum_fusion.turned_ref, bf16[512,1344]{1,0:T(8,128)(2,1)} %get-tuple-element.31.delta_ref, ...), custom_call_target="tpu_custom_call" | custom-call | flops 10000000000 | bytes 50000000 | tf_op jit(solution)/shard_map/pallas_call | solution.py:473
  290.0 5.2 %copy.40 = bf16[2048,1280]{1,0:T(8,128)(2,1)} copy(bf16[2048,1280]{1,0:T(8,128)(2,1)} %get-tuple-element.59) | data formatting | bytes 10485760
  295.3 0.6 copy.41
  295.9 0.6 copy.42
  (19 shorter events, 0.2 us)
Async XLA Ops:
  19.4 12.9 %copy-start.6 = (s32[2048]{0:T(1024)S(1)}, s32[2048]{0:T(1024)}, u32[]{:S(2)}) copy-start(s32[2048]{0:T(1024)} %param.13) | copy-start | bytes 24580
  19.5 82.2 %all-to-all-start = ((bf16[64,32,1344]{2,1,0:T(8,128)(2,1)}), bf16[64,32,1344]{2,1,0:T(8,128)(2,1)}, u32[]{:S(2)}, u32[]{:S(2)}) async-start(bf16[64,32,1344]{2,1,0:T(8,128)(2,1)} %bitcast.27), calls=%async_computation | async-start | bytes 11534336 | tf_op jit(solution)/shard_map/all_to_all | solution.py:526
  34.2 3.0 %copy-start.4 = (s32[2048]{0:T(1024)}, s32[2048]{0:T(1024)S(1)}, u32[]{:S(2)}) copy-start(s32[2048]{0:T(1024)S(1)} %convert_reduce_fusion) | copy-start | bytes 24580
  101.6 14.8 %copy-start = (bf16[1024,1280]{1,0:T(8,128)(2,1)S(1)}, bf16[1024,1280]{1,0:T(8,128)(2,1)}, u32[]{:S(2)}) copy-start(bf16[1024,1280]{1,0:T(8,128)(2,1)} %get-tuple-element.19.bf_ref) | copy-start | bytes 7864324
  101.6 83.3 %all-to-all-start.1 = ((bf16[64,32,1344]{2,1,0:T(8,128)(2,1)}), bf16[64,32,1344]{2,1,0:T(8,128)(2,1)}, u32[]{:S(2)}, u32[]{:S(2)}) async-start(bf16[64,32,1344]{2,1,0:T(8,128)(2,1)} %bitcast.28), calls=%async_computation.1 | async-start | bytes 11534336 | tf_op jit(solution)/shard_map/all_to_all | solution.py:526
  119.2 45.8 %copy-start.1 = (bf16[1024,1280]{0,1:T(8,128)(2,1)S(1)}, bf16[1024,1280]{0,1:T(8,128)(2,1)}, u32[]{:S(2)}) copy-start(bf16[1024,1280]{0,1:T(8,128)(2,1)} %copy.32) | copy-start | bytes 7864324
  163.3 2.1 copy-start.5
  163.3 66.5 %collective-permute-start = (bf16[512,1280]{1,0:T(8,128)(2,1)}, bf16[512,1280]{1,0:T(8,128)(2,1)}, u32[]{:S(2)}, u32[]{:S(2)}) collective-permute-start(bf16[512,1280]{1,0:T(8,128)(2,1)} %get-tuple-element.33.grad0_ref), channel_id=1, source_target_pairs={{0,64},{64,0},{1,65},{65,1},{2,66},{66,2},{3,67},{67,3},{4,68},{68... | collective-permute-start | bytes 3932168 | tf_op jit(solution)/shard_map/ppermute | solution.py:573
  290.0 5.2 %copy-start.2 = (f32[40,768]{1,0:T(8,128)S(1)}, f32[40,768]{1,0:T(8,128)}, u32[]{:S(2)}) copy-start(f32[40,768]{1,0:T(8,128)} %get-tuple-element.60) | copy-start | bytes 368644
  290.0 5.9 %copy-start.3 = (f32[40,576]{1,0:T(8,128)S(1)}, f32[40,576]{1,0:T(8,128)}, u32[]{:S(2)}) copy-start(f32[40,576]{1,0:T(8,128)} %get-tuple-element.61) | copy-start | bytes 276484

commit v5 on v4

--- a/solution.py
+++ b/solution.py
@@ -333,10 +333,11 @@
     return {"tsec": x % 2, "dp": (y * 4 + z) * 2 + c, "rep": x // 2}
 
 
-def tail_kernel(scale, part_ref, turned_ref, delta_ref, delta_far_ref, rank_ref, grad0_ref, grad0_far_ref, grad1_ref,
-                feature_ref, dino_ref, siglip_ref,
+def tail_kernel(scale, part_ref, turned_ref, delta_ref, delta_far_ref, rank_ref, grad0_in, grad0_far_in, grad1_in,
+                feature_out, dino_ref, siglip_ref,
                 work, pair, far_y, far_z, far_y2, far_z2, far_x, stage, grad1_far,
-                load_sem, pair_send, pair_recv, send_sem, recv_sem):
+                load_sem, pair_send, pair_recv, send_sem, recv_sem,
+                feature_ref, grad0_ref, grad0_far_ref, grad1_ref, grad_sem, out_sem):
     x, y, z, c = place()
     t = x % 2
     sibling, partner = at_place(x, y, z, 1 - c), {"tsec": 1 - t}
@@ -352,10 +353,20 @@
 
     for h, j in steps:
         load(h, j).start()
+    grad_loads = [
+        pltpu.make_async_copy(src, dst, grad_sem.at[i])
+        for i, (src, dst) in enumerate(
+            ((grad0_in, grad0_ref), (grad0_far_in, grad0_far_ref), (grad1_in, grad1_ref)))]
+    for copy in grad_loads:
+        copy.start()
+
+    def store(i):
+        return pltpu.make_async_copy(feature_ref.at[tile_at(i)], feature_out.at[tile_at(i)], out_sem.at[i])
+
     lines = [[at_place(x, (y + j) % 4, z, c), at_place(x, y, (z + j) % 4, c), at_place((x + j) % 4, y, z, c)]
              for j in (1, 2, 3)]
     greet([sibling] + sum(lines, []))
-    back = remote(grad1_ref, grad1_far, send_sem.at[15], recv_sem.at[15], partner)
+    back = remote(grad1_in, grad1_far, send_sem.at[15], recv_sem.at[15], partner)
     back.start()
     rows = feature_ref.shape[1] // 32
 
@@ -402,6 +413,9 @@
     for h, j in steps[-lag:]:
         combine(h, j)
 
+    for copy in grad_loads:
+        copy.wait()
+
     count = grad0_ref.shape[0]
     starts = [(2 * s + side) * count for s in (0, 1) for side in (t, 1 - t)]
 
@@ -443,6 +457,7 @@
         hit = hits(rank_ref[tile_at(i)], starts[3], count)
         found = jnp.dot(hit, grad1_far[...], preferred_element_type=F32)
         feature_ref[tile_at(i)] = (feature_ref[tile_at(i)].astype(F32) + found).astype(BF)
+        store(i).start()
 
     for h in (0, 1):
         far = far_z2 if h == 0 else far_y2
@@ -462,6 +477,10 @@
     for j in (2, 1, 3):
         x_copy(j).wait()
     total = (stage[0].astype(F32) + far_x[0].astype(F32) + far_x[1].astype(F32) + far_x[2].astype(F32)) * scale
+    @pl.loop(0, feature_ref.shape[0] // TILE)
+    def _(i):
+        store(i).wait()
+
     dino_ref[...] = total[:rows, : dino_ref.shape[1]]
     siglip_ref[...] = total[:rows, dino_ref.shape[1] :]
 
@@ -476,8 +495,8 @@
             jax.ShapeDtypeStruct((rank.shape[0], features), BF),
             jax.ShapeDtypeStruct((own_rows, dino_cols), F32),
             jax.ShapeDtypeStruct((own_rows, block[1] - dino_cols), F32)],
-        in_specs=[HERE] + [VMEM] * 7,
-        out_specs=[VMEM] * 3,
+        in_specs=[HERE] + [VMEM] * 4 + [HERE] * 3,
+        out_specs=[HERE] + [VMEM] * 2,
         scratch_shapes=[
             pltpu.VMEM((2, 4, 4, 2) + block, BF),
             pltpu.VMEM((2, 4, 4) + block, BF),
@@ -493,7 +512,10 @@
             pltpu.SemaphoreType.DMA((8,)),
             pltpu.SemaphoreType.DMA((16,)),
             pltpu.SemaphoreType.DMA((16,)),
-        ],
+            pltpu.VMEM((rank.shape[0], features), BF),
+        ]
+        + [pltpu.VMEM((count, features), BF)] * 3
+        + [pltpu.SemaphoreType.DMA((3,)), pltpu.SemaphoreType.DMA((rank.shape[0] // TILE,))],
         compiler_params=pltpu.CompilerParams(
             collective_id=0, has_side_effects=True, vmem_limit_bytes=60 * 2**20
         ),

time: 300 us -> 298 us (level)
  Pallas kernels: 237 us -> 234 us
where the time goes in v5:
time: 298 us; the launch traced here: 294 us
  Pallas kernels  234 us (79%)
  starting transfers between devices  28.2 us (9%)
  local copies, waits for them, and re-layouts  13.1 us (4%)
  waiting for transfers between devices  11 us (4%)
  other arithmetic  6.88 us (2%)
    pallas_call x2, Pallas kernels, handle_block(): pl.pallas_call(functools.partial(block_kernel, stage), in_specs=[VMEM] *...  88.9 us
    pallas_call x1, Pallas kernels, forward(): pl.pallas_call(forward_kernel, in_specs=[VMEM] * 8 + [HERE], out_specs=[V...  61.2 us
    pallas_call x1, Pallas kernels, finish(): pl.pallas_call(functools.partial(tail_kernel, scale), out_shape=[jax.Shap...  57.6 us
    all_to_all x2, starting transfers between devices, exchange(): lax.all_to_all(outbox.reshape(groups, CHUNKS[chunk][1], -1), ('tsec', 'dp...  26.4 us
    pallas_call x1, Pallas kernels, local_call(): pl.pallas_call(kernel, grid=(steps,), in_specs=in_specs, out_specs=out_sp...  17.5 us
    all_to_all x2, waiting for transfers between devices, exchange(): lax.all_to_all(outbox.reshape(groups, CHUNKS[chunk][1], -1), ('tsec', 'dp...  11 us
    pallas_call x1, Pallas kernels, wgrad_part(): pl.pallas_call(functools.partial(wgrad_kernel, len(deltas)), grid=(split,...  8.75 us
    unnamed x17, local copies, waits for them, and re-layouts  6.55 us
  transfers between devices with their start and end apart: 3, of which 2 were waited for; matrix products, arithmetic and copies ran while one was open for 4% of the time, Pallas kernels for 54%

profile of v5, /device:TPU:1, one launch (start us, length us, event | category | flops | bytes accessed | tf_op | source)
XLA Modules:
  0.0 294.1 jit_solution(4063210316304009214)
XLA Ops:
  0.6 1.3 add_select_fusion.4
  1.9 17.5 %shard_map.94.after_ref = bf16[2048,1344]{1,0:T(8,128)(2,1)} custom-call(s32[1,2048]{1,0:T(1,128)} %bitcast.36, bf16[2048,768]{1,0:T(8,128)(2,1)} %dino_feat_ref.1, bf16[576,2048]{1,0:T(8,128)(2,1)} %bitcast.31, s32[2048]{0:T(1024)} %after_ref.1), custom_call_target="tpu_custom_call" | custom-call | flops 1048576 | bytes 65536 | tf_op jit(solution)/shard_map/pallas_call | solution.py:39
  19.5 12.8 %all-to-all-start = ((bf16[64,32,1344]{2,1,0:T(8,128)(2,1)}), bf16[64,32,1344]{2,1,0:T(8,128)(2,1)}, u32[]{:S(2)}, u32[]{:S(2)}) async-start(bf16[64,32,1344]{2,1,0:T(8,128)(2,1)} %bitcast.27), calls=%async_computation | async-start | bytes 11534336 | tf_op jit(solution)/shard_map/all_to_all | solution.py:548
  32.4 1.8 convert_reduce_fusion
  34.2 0.0 copy-start.4
  34.2 1.7 select_reduce_fusion
  35.9 0.1 fusion.11
  36.1 1.0 copy.29.columns_ref
  37.2 61.2 %shard_map.95 = (f32[1024,1280]{1,0:T(8,128)}, bf16[1024,1280]{1,0:T(8,128)(2,1)}, f32[1024,1]{1,0:T(8,128)}, f32[1024,1344]{1,0:T(8,128)}, f32[1024,1344]{1,0:T...) custom-call(s32[1024,4]{1,0:T(8,128)} %copy.29.columns_ref, ...), custom_call_target="tpu_custom_call" | custom-call | flops 30000001024 | bytes 50000000 | tf_op jit(solution)/shard_map/pallas_call | solution.py:154
  98.4 3.2 %all-to-all-done = bf16[64,32,1344]{2,1,0:T(8,128)(2,1)} async-done(((bf16[64,32,1344]{2,1,0:T(8,128)(2,1)}), bf16[64,32,1344]{2,1,0:T(8,128)(2,1)}, u32[]{:S(2)}, u32[]{:S(2)}) %all-to-all-start) | async-done | bytes 5505056 | tf_op jit(solution)/shard_map/all_to_all | solution.py:548
  101.6 13.6 %all-to-all-start.1 = ((bf16[64,32,1344]{2,1,0:T(8,128)(2,1)}), bf16[64,32,1344]{2,1,0:T(8,128)(2,1)}, u32[]{:S(2)}, u32[]{:S(2)}) async-start(bf16[64,32,1344]{2,1,0:T(8,128)(2,1)} %bitcast.28), calls=%async_computation.1 | async-start | bytes 11534336 | tf_op jit(solution)/shard_map/all_to_all | solution.py:548
  115.4 1.0 copy.31.columns_far_ref
  116.4 0.0 copy-done
  116.4 2.8 copy.32
  119.2 0.0 copy-start.1
  119.2 44.0 %shard_map.96 = (bf16[512,1344]{1,0:T(8,128)(2,1)}, bf16[512,1344]{1,0:T(8,128)(2,1)}, bf16[512,1280]{1,0:T(8,128)(2,1)}, bf16[512,1344]{1,0:T(8,128)(2,1)}, bf16[512,1344]{1,0:T(8,128)(2,1)}) custom-call(s32[1024,4]{1,0:T(8,128)} %copy.29.columns_ref, s32[1024,4]{1,0:T(8,128)} %copy.31.columns_far_ref, f32[1024,1]{1,0:T(8,128)} %get-tuple-element.20.inv_ref, ...), custom_call_target="tpu_custom_call" | custom-call | flops 10000000000 | bytes 30000000 | tf_op jit(solution)/shard_map/pallas_call | solution.py:272
  163.3 0.0 copy-start.5
  163.3 1.7 collective-permute-start
  165.0 0.2 slice_bitcast_fusion
  165.2 0.1 copy.33
  165.4 1.4 copy.36.rank_ref
  166.7 1.7 pad_maximum_fusion.turned_ref
  168.4 8.7 %shard_map.97.refs_2_ = bf16[2,32,48,1344]{3,2,1,0:T(8,128)(2,1)} custom-call(bf16[1024,1280]{1,0:T(8,128)(2,1)} %get-tuple-element.19.bf_ref, bf16[512,1344]{1,0:T(8,128)(2,1)} %get-tuple-element.26.refs_0_, bf16[512,1344]{1,0:T(8,128)(2,1)} %get-tuple-element.27.refs_1_), custom_call_target="tpu_custom_call" | custom-call | flops 1048576 | bytes 65536 | tf_op jit(solution)/shard_map/pallas_call | solution.py:314
  177.2 7.7 %all-to-all-done.1 = bf16[64,32,1344]{2,1,0:T(8,128)(2,1)} async-done(((bf16[64,32,1344]{2,1,0:T(8,128)(2,1)}), bf16[64,32,1344]{2,1,0:T(8,128)(2,1)}, u32[]{:S(2)}, u32[]{:S(2)}) %all-to-all-start.1) | async-done | bytes 5505056 | tf_op jit(solution)/shard_map/all_to_all | solution.py:548
  184.9 44.9 %shard_map.98 = (bf16[512,1344]{1,0:T(8,128)(2,1)}, bf16[512,1344]{1,0:T(8,128)(2,1)}, bf16[512,1280]{1,0:T(8,128)(2,1)}) custom-call(s32[1024,4]{1,0:T(8,128)} %copy.29.columns_ref, s32[1024,4]{1,0:T(8,128)} %copy.31.columns_far_ref, f32[1024,1]{1,0:T(8,128)} %get-tuple-element.20.inv_ref, bf16[2048,1344]{1,0:T(8,128)(2,1)} %bitcast.20.inbox_ref, ...), custom_call_target="tpu_custom_call" | custom-call | flops 10000000000 | bytes 30000000 | tf_op jit(solution)/shard_map/pallas_call | solution.py:272
  229.8 0.0 collective-permute-done.grad0_far_in
  229.8 57.6 %shard_map.99 = (bf16[2048,1280]{1,0:T(8,128)(2,1)}, f32[40,768]{1,0:T(8,128)}, f32[40,576]{1,0:T(8,128)}) custom-call(bf16[2,4,4,2,48,1344]{5,4,3,2,1,0:T(8,128)(2,1)} %bitcast.26, bf16[2,1280,512]{2,1,0:T(8,128)(2,1)} %pad_maximum_fusion.turned_ref, bf16[512,1344]{1,0:T(8,128)(2,1)} %get-tuple-element.31.delta_ref, ...), custom_call_target="tpu_custom_call" | custom-call | flops 10000000000 | bytes 50000000 | tf_op jit(solution)/shard_map/pallas_call | solution.py:492
  287.4 5.2 %copy.40 = bf16[2048,1280]{1,0:T(8,128)(2,1)} copy(bf16[2048,1280]{1,0:T(8,128)(2,1)} %get-tuple-element.59) | data formatting | bytes 10485760
  292.6 0.0 copy-done.2
  292.6 0.6 copy.41
  293.3 0.0 copy-done.3
  293.3 0.6 copy.42
  (19 shorter events, 0.2 us)
Async XLA Ops:
  19.4 12.9 %copy-start.6 = (s32[2048]{0:T(1024)S(1)}, s32[2048]{0:T(1024)}, u32[]{:S(2)}) copy-start(s32[2048]{0:T(1024)} %param.13) | copy-start | bytes 24580
  19.5 82.2 %all-to-all-start = ((bf16[64,32,1344]{2,1,0:T(8,128)(2,1)}), bf16[64,32,1344]{2,1,0:T(8,128)(2,1)}, u32[]{:S(2)}, u32[]{:S(2)}) async-start(bf16[64,32,1344]{2,1,0:T(8,128)(2,1)} %bitcast.27), calls=%async_computation | async-start | bytes 11534336 | tf_op jit(solution)/shard_map/all_to_all | solution.py:548
  34.2 3.0 %copy-start.4 = (s32[2048]{0:T(1024)}, s32[2048]{0:T(1024)S(1)}, u32[]{:S(2)}) copy-start(s32[2048]{0:T(1024)S(1)} %convert_reduce_fusion) | copy-start | bytes 24580
  101.6 14.8 %copy-start = (bf16[1024,1280]{1,0:T(8,128)(2,1)S(1)}, bf16[1024,1280]{1,0:T(8,128)(2,1)}, u32[]{:S(2)}) copy-start(bf16[1024,1280]{1,0:T(8,128)(2,1)} %get-tuple-element.19.bf_ref) | copy-start | bytes 7864324
  101.6 83.3 %all-to-all-start.1 = ((bf16[64,32,1344]{2,1,0:T(8,128)(2,1)}), bf16[64,32,1344]{2,1,0:T(8,128)(2,1)}, u32[]{:S(2)}, u32[]{:S(2)}) async-start(bf16[64,32,1344]{2,1,0:T(8,128)(2,1)} %bitcast.28), calls=%async_computation.1 | async-start | bytes 11534336 | tf_op jit(solution)/shard_map/all_to_all | solution.py:548
  119.2 45.8 %copy-start.1 = (bf16[1024,1280]{0,1:T(8,128)(2,1)S(1)}, bf16[1024,1280]{0,1:T(8,128)(2,1)}, u32[]{:S(2)}) copy-start(bf16[1024,1280]{0,1:T(8,128)(2,1)} %copy.32) | copy-start | bytes 7864324
  163.3 2.1 copy-start.5
  163.3 66.5 %collective-permute-start = (bf16[512,1280]{1,0:T(8,128)(2,1)}, bf16[512,1280]{1,0:T(8,128)(2,1)}, u32[]{:S(2)}, u32[]{:S(2)}) collective-permute-start(bf16[512,1280]{1,0:T(8,128)(2,1)} %get-tuple-element.33.grad0_in), channel_id=1, source_target_pairs={{0,64},{64,0},{1,65},{65,1},{2,66},{66,2},{3,67},{67,3},{4,68},{68... | collective-permute-start | bytes 3932168 | tf_op jit(solution)/shard_map/ppermute | solution.py:595
  287.4 5.2 %copy-start.2 = (f32[40,768]{1,0:T(8,128)S(1)}, f32[40,768]{1,0:T(8,128)}, u32[]{:S(2)}) copy-start(f32[40,768]{1,0:T(8,128)} %get-tuple-element.60) | copy-start | bytes 368644
  287.4 5.9 %copy-start.3 = (f32[40,576]{1,0:T(8,128)S(1)}, f32[40,576]{1,0:T(8,128)}, u32[]{:S(2)}) copy-start(f32[40,576]{1,0:T(8,128)} %get-tuple-element.61) | copy-start | bytes 276484

commit v6 on v5

--- a/solution.py
+++ b/solution.py
@@ -206,7 +206,7 @@
             (siglip_far_ref, siglip_far_w), (out_ref.at[pl.ds(first, rows)], out),
             (out_far_ref.at[pl.ds(first, rows)], out_far), (normed_ref.at[pl.ds(first, rows)], normed_all)))
     ]
-    for load in loads:
+    for load in loads[: 1 + len(bases)]:
         load.start()
     partner = {"tsec": 1 - lax.axis_index("tsec")}
     greet([partner])
@@ -220,6 +220,8 @@
 
     for load in loads[: 1 + len(bases)]:
         load.wait()
+    for load in loads[1 + len(bases) :]:
+        load.start()
     steps = rows // tile
     for i in range(steps):
         found = look_up(columns_far_ref[at(i, first), 2 + stage : 3 + stage])
@@ -357,9 +359,6 @@
         pltpu.make_async_copy(src, dst, grad_sem.at[i])
         for i, (src, dst) in enumerate(
             ((grad0_in, grad0_ref), (grad0_far_in, grad0_far_ref), (grad1_in, grad1_ref)))]
-    for copy in grad_loads:
-        copy.start()
-
     def store(i):
         return pltpu.make_async_copy(feature_ref.at[tile_at(i)], feature_out.at[tile_at(i)], out_sem.at[i])
 
@@ -410,6 +409,8 @@
         pair_copy(h, j).start()
         if i >= lag:
             combine(*steps[i - lag])
+    for copy in grad_loads:
+        copy.start()
     for h, j in steps[-lag:]:
         combine(h, j)
 

time: 298 us -> 298 us (level)
  no operation moved by 1% of the time
where the time goes in v6:
time: 298 us; the launch traced here: 294 us
  Pallas kernels  234 us (79%)
  starting transfers between devices  28.2 us (9%)
  local copies, waits for them, and re-layouts  13.1 us (4%)
  waiting for transfers between devices  11 us (4%)
  other arithmetic  6.88 us (2%)
    pallas_call x2, Pallas kernels, handle_block(): pl.pallas_call(functools.partial(block_kernel, stage), in_specs=[VMEM] *...  88.9 us
    pallas_call x1, Pallas kernels, forward(): pl.pallas_call(forward_kernel, in_specs=[VMEM] * 8 + [HERE], out_specs=[V...  61.2 us
    pallas_call x1, Pallas kernels, finish(): pl.pallas_call(functools.partial(tail_kernel, scale), out_shape=[jax.Shap...  57.6 us
    all_to_all x2, starting transfers between devices, exchange(): lax.all_to_all(outbox.reshape(groups, CHUNKS[chunk][1], -1), ('tsec', 'dp...  26.4 us
    pallas_call x1, Pallas kernels, local_call(): pl.pallas_call(kernel, grid=(steps,), in_specs=in_specs, out_specs=out_sp...  17.5 us
    all_to_all x2, waiting for transfers between devices, exchange(): lax.all_to_all(outbox.reshape(groups, CHUNKS[chunk][1], -1), ('tsec', 'dp...  11 us
    pallas_call x1, Pallas kernels, wgrad_part(): pl.pallas_call(functools.partial(wgrad_kernel, len(deltas)), grid=(split,...  8.75 us
    unnamed x17, local copies, waits for them, and re-layouts  6.55 us
  transfers between devices with their start and end apart: 3, of which 2 were waited for; matrix products, arithmetic and copies ran while one was open for 4% of the time, Pallas kernels for 54%

profile of v6, /device:TPU:1, one launch (start us, length us, event | category | flops | bytes accessed | tf_op | source)
XLA Modules:
  0.0 294.1 jit_solution(1187932156513997211)
XLA Ops:
  0.6 1.3 add_select_fusion.4
  1.9 17.5 %shard_map.94.after_ref = bf16[2048,1344]{1,0:T(8,128)(2,1)} custom-call(s32[1,2048]{1,0:T(1,128)} %bitcast.36, bf16[2048,768]{1,0:T(8,128)(2,1)} %dino_feat_ref.1, bf16[576,2048]{1,0:T(8,128)(2,1)} %bitcast.31, s32[2048]{0:T(1024)} %after_ref.1), custom_call_target="tpu_custom_call" | custom-call | flops 1048576 | bytes 65536 | tf_op jit(solution)/shard_map/pallas_call | solution.py:39
  19.5 12.8 %all-to-all-start = ((bf16[64,32,1344]{2,1,0:T(8,128)(2,1)}), bf16[64,32,1344]{2,1,0:T(8,128)(2,1)}, u32[]{:S(2)}, u32[]{:S(2)}) async-start(bf16[64,32,1344]{2,1,0:T(8,128)(2,1)} %bitcast.27), calls=%async_computation | async-start | bytes 11534336 | tf_op jit(solution)/shard_map/all_to_all | solution.py:549
  32.4 1.8 convert_reduce_fusion
  34.2 0.0 copy-start.4
  34.2 1.7 select_reduce_fusion
  35.9 0.1 fusion.11
  36.1 1.0 copy.29.columns_ref
  37.2 61.2 %shard_map.95 = (f32[1024,1280]{1,0:T(8,128)}, bf16[1024,1280]{1,0:T(8,128)(2,1)}, f32[1024,1]{1,0:T(8,128)}, f32[1024,1344]{1,0:T(8,128)}, f32[1024,1344]{1,0:T...) custom-call(s32[1024,4]{1,0:T(8,128)} %copy.29.columns_ref, ...), custom_call_target="tpu_custom_call" | custom-call | flops 30000001024 | bytes 50000000 | tf_op jit(solution)/shard_map/pallas_call | solution.py:154
  98.4 3.2 %all-to-all-done = bf16[64,32,1344]{2,1,0:T(8,128)(2,1)} async-done(((bf16[64,32,1344]{2,1,0:T(8,128)(2,1)}), bf16[64,32,1344]{2,1,0:T(8,128)(2,1)}, u32[]{:S(2)}, u32[]{:S(2)}) %all-to-all-start) | async-done | bytes 5505056 | tf_op jit(solution)/shard_map/all_to_all | solution.py:549
  101.6 13.6 %all-to-all-start.1 = ((bf16[64,32,1344]{2,1,0:T(8,128)(2,1)}), bf16[64,32,1344]{2,1,0:T(8,128)(2,1)}, u32[]{:S(2)}, u32[]{:S(2)}) async-start(bf16[64,32,1344]{2,1,0:T(8,128)(2,1)} %bitcast.28), calls=%async_computation.1 | async-start | bytes 11534336 | tf_op jit(solution)/shard_map/all_to_all | solution.py:549
  115.4 1.0 copy.31.columns_far_ref
  116.4 0.0 copy-done
  116.4 2.8 copy.32
  119.2 0.0 copy-start.1
  119.2 44.0 %shard_map.96 = (bf16[512,1344]{1,0:T(8,128)(2,1)}, bf16[512,1344]{1,0:T(8,128)(2,1)}, bf16[512,1280]{1,0:T(8,128)(2,1)}, bf16[512,1344]{1,0:T(8,128)(2,1)}, bf16[512,1344]{1,0:T(8,128)(2,1)}) custom-call(s32[1024,4]{1,0:T(8,128)} %copy.29.columns_ref, s32[1024,4]{1,0:T(8,128)} %copy.31.columns_far_ref, f32[1024,1]{1,0:T(8,128)} %get-tuple-element.20.inv_ref, ...), custom_call_target="tpu_custom_call" | custom-call | flops 10000000000 | bytes 30000000 | tf_op jit(solution)/shard_map/pallas_call | solution.py:274
  163.3 0.0 copy-start.5
  163.3 1.7 collective-permute-start
  165.0 0.0 copy-done.1
  165.0 0.2 slice_bitcast_fusion
  165.2 0.1 copy.33
  165.4 0.0 copy-done.5
  165.4 1.4 copy.36.rank_ref
  166.7 1.7 pad_maximum_fusion.turned_ref
  168.4 8.7 %shard_map.97.refs_2_ = bf16[2,32,48,1344]{3,2,1,0:T(8,128)(2,1)} custom-call(bf16[1024,1280]{1,0:T(8,128)(2,1)} %get-tuple-element.19.bf_ref, bf16[512,1344]{1,0:T(8,128)(2,1)} %get-tuple-element.26.refs_0_, bf16[512,1344]{1,0:T(8,128)(2,1)} %get-tuple-element.27.refs_1_), custom_call_target="tpu_custom_call" | custom-call | flops 1048576 | bytes 65536 | tf_op jit(solution)/shard_map/pallas_call | solution.py:316
  177.2 7.7 %all-to-all-done.1 = bf16[64,32,1344]{2,1,0:T(8,128)(2,1)} async-done(((bf16[64,32,1344]{2,1,0:T(8,128)(2,1)}), bf16[64,32,1344]{2,1,0:T(8,128)(2,1)}, u32[]{:S(2)}, u32[]{:S(2)}) %all-to-all-start.1) | async-done | bytes 5505056 | tf_op jit(solution)/shard_map/all_to_all | solution.py:549
  184.9 44.9 %shard_map.98 = (bf16[512,1344]{1,0:T(8,128)(2,1)}, bf16[512,1344]{1,0:T(8,128)(2,1)}, bf16[512,1280]{1,0:T(8,128)(2,1)}) custom-call(s32[1024,4]{1,0:T(8,128)} %copy.29.columns_ref, s32[1024,4]{1,0:T(8,128)} %copy.31.columns_far_ref, f32[1024,1]{1,0:T(8,128)} %get-tuple-element.20.inv_ref, bf16[2048,1344]{1,0:T(8,128)(2,1)} %bitcast.20.inbox_ref, ...), custom_call_target="tpu_custom_call" | custom-call | flops 10000000000 | bytes 30000000 | tf_op jit(solution)/shard_map/pallas_call | solution.py:274
  229.8 0.0 collective-permute-done.grad0_far_in
  229.8 57.6 %shard_map.99 = (bf16[2048,1280]{1,0:T(8,128)(2,1)}, f32[40,768]{1,0:T(8,128)}, f32[40,576]{1,0:T(8,128)}) custom-call(bf16[2,4,4,2,48,1344]{5,4,3,2,1,0:T(8,128)(2,1)} %bitcast.26, bf16[2,1280,512]{2,1,0:T(8,128)(2,1)} %pad_maximum_fusion.turned_ref, bf16[512,1344]{1,0:T(8,128)(2,1)} %get-tuple-element.31.delta_ref, ...), custom_call_target="tpu_custom_call" | custom-call | flops 10000000000 | bytes 50000000 | tf_op jit(solution)/shard_map/pallas_call | solution.py:493
  287.4 5.2 %copy.40 = bf16[2048,1280]{1,0:T(8,128)(2,1)} copy(bf16[2048,1280]{1,0:T(8,128)(2,1)} %get-tuple-element.59) | data formatting | bytes 10485760
  292.6 0.6 copy.41
  293.3 0.6 copy.42
  (19 shorter events, 0.2 us)
Async XLA Ops:
  19.4 12.9 %copy-start.6 = (s32[2048]{0:T(1024)S(1)}, s32[2048]{0:T(1024)}, u32[]{:S(2)}) copy-start(s32[2048]{0:T(1024)} %param.13) | copy-start | bytes 24580
  19.5 82.2 %all-to-all-start = ((bf16[64,32,1344]{2,1,0:T(8,128)(2,1)}), bf16[64,32,1344]{2,1,0:T(8,128)(2,1)}, u32[]{:S(2)}, u32[]{:S(2)}) async-start(bf16[64,32,1344]{2,1,0:T(8,128)(2,1)} %bitcast.27), calls=%async_computation | async-start | bytes 11534336 | tf_op jit(solution)/shard_map/all_to_all | solution.py:549
  34.2 3.0 %copy-start.4 = (s32[2048]{0:T(1024)}, s32[2048]{0:T(1024)S(1)}, u32[]{:S(2)}) copy-start(s32[2048]{0:T(1024)S(1)} %convert_reduce_fusion) | copy-start | bytes 24580
  101.6 14.8 %copy-start = (bf16[1024,1280]{1,0:T(8,128)(2,1)S(1)}, bf16[1024,1280]{1,0:T(8,128)(2,1)}, u32[]{:S(2)}) copy-start(bf16[1024,1280]{1,0:T(8,128)(2,1)} %get-tuple-element.19.bf_ref) | copy-start | bytes 7864324
  101.6 83.3 %all-to-all-start.1 = ((bf16[64,32,1344]{2,1,0:T(8,128)(2,1)}), bf16[64,32,1344]{2,1,0:T(8,128)(2,1)}, u32[]{:S(2)}, u32[]{:S(2)}) async-start(bf16[64,32,1344]{2,1,0:T(8,128)(2,1)} %bitcast.28), calls=%async_computation.1 | async-start | bytes 11534336 | tf_op jit(solution)/shard_map/all_to_all | solution.py:549
  119.2 45.8 %copy-start.1 = (bf16[1024,1280]{0,1:T(8,128)(2,1)S(1)}, bf16[1024,1280]{0,1:T(8,128)(2,1)}, u32[]{:S(2)}) copy-start(bf16[1024,1280]{0,1:T(8,128)(2,1)} %copy.32) | copy-start | bytes 7864324
  163.3 2.1 copy-start.5
  163.3 66.5 %collective-permute-start = (bf16[512,1280]{1,0:T(8,128)(2,1)}, bf16[512,1280]{1,0:T(8,128)(2,1)}, u32[]{:S(2)}, u32[]{:S(2)}) collective-permute-start(bf16[512,1280]{1,0:T(8,128)(2,1)} %get-tuple-element.33.grad0_in), channel_id=1, source_target_pairs={{0,64},{64,0},{1,65},{65,1},{2,66},{66,2},{3,67},{67,3},{4,68},{68... | collective-permute-start | bytes 3932168 | tf_op jit(solution)/shard_map/ppermute | solution.py:596
  287.4 5.2 %copy-start.2 = (f32[40,768]{1,0:T(8,128)S(1)}, f32[40,768]{1,0:T(8,128)}, u32[]{:S(2)}) copy-start(f32[40,768]{1,0:T(8,128)} %get-tuple-element.60) | copy-start | bytes 368644
  287.4 5.9 %copy-start.3 = (f32[40,576]{1,0:T(8,128)S(1)}, f32[40,576]{1,0:T(8,128)}, u32[]{:S(2)}) copy-start(f32[40,576]{1,0:T(8,128)} %get-tuple-element.61) | copy-start | bytes 276484
